TPU v7x, 256 devices: a whole 4x4x8 slice. The times are simulated.
256 devices in a mesh: wide: 32 (over y_hi, z, core), narrow: 8 (over x, y_lo).
Axes of the slice: x: 4, y: 4 (y_hi: 2, y_lo: 2; y = y_hi * 2 + y_lo), z: 8, core: 2. Of those that a mesh axis runs over, the one named last changes fastest.
Arguments:
- head_table: float32 [32768, 400], P('wide'), may hold values from -1.5 to 1.5
- head_state: float32 [32768], P('wide'), may hold values from 0.0001 to 1
- tail_table: float32 [131072, 400], P(('wide', 'narrow')), may hold values from -1.5 to 1.5
- tail_state: float32 [131072], P(('wide', 'narrow')), may hold values from 0.0001 to 1
- relations: bfloat16 [7424, 400], replicated, may hold values from -4 to 4
- head_rows: int32 [2, 262144], P(None, ('wide', 'narrow')), may hold values from 0 to 1023
- tail_rows: int32 [2, 262144], P(None, ('wide', 'narrow')), may hold values from 0 to 511
- relation_ids: int32 [2, 262144], P(None, ('wide', 'narrow')), may hold values from 0 to 7423
Outputs:
- new_head_table: float32 [32768, 400], P('wide')
- new_head_state: float32 [32768], P('wide')
- new_tail_table: float32 [131072, 400], P(('wide', 'narrow'))
- new_tail_state: float32 [131072], P(('wide', 'narrow'))
All inputs are finite; a program needn't handle non-finite values.
Results may differ from a plain program's by a relative error of at most 0.01.
Values may be sent and summed in bfloat16 or wider, within the bound.
No kernel may reach another device: no remote copies, remote signals or barrier semaphores. Data moves between devices by JAX's collectives and lax.ppermute only.
A program may use at most 64 MiB of HBM per device.

v0:
```python
import jax
import jax.numpy as jnp
from jax import lax
from jax.sharding import PartitionSpec as P

learning = 0.1


def passed_along(value, axis, steps):
    count = lax.axis_size(axis)
    pairs = [(source, (source + steps) % count) for source in range(count)]
    return lax.ppermute(value, axis, pairs)


def complex_product(first, second):
    half_width = first.shape[-1] // 2
    first_real, first_imag = (first[..., :half_width], first[..., half_width:])
    second_real, second_imag = (second[..., :half_width], second[..., half_width:])
    return jnp.concatenate(
        [
            first_real * second_real - first_imag * second_imag,
            first_real * second_imag + first_imag * second_real,
        ],
        axis=-1,
    )


def conj_product(first, second):
    half_width = first.shape[-1] // 2
    first_real, first_imag = (first[..., :half_width], first[..., half_width:])
    second_real, second_imag = (second[..., :half_width], second[..., half_width:])
    return jnp.concatenate(
        [
            first_real * second_real + first_imag * second_imag,
            first_imag * second_real - first_real * second_imag,
        ],
        axis=-1,
    )


def adagrad(table, state, grad):
    state_new = state + jnp.mean(grad * grad, axis=1)
    return (table - learning * grad / jnp.sqrt(state_new)[:, None], state_new)


def edge_terms(queries, span, tail_idx):
    span_low = span.astype(jnp.bfloat16)
    row_count = span.shape[0]
    scores = jnp.dot(queries, span_low.T, preferred_element_type=jnp.float32)
    positive = tail_idx[:, None] == jnp.arange(row_count, dtype=jnp.int32)[None, :]
    slopes = jax.nn.sigmoid(scores) / row_count - jnp.where(positive, jax.nn.sigmoid(-scores), 0.0)
    slopes = slopes.astype(jnp.bfloat16)
    tail_grad = jnp.dot(slopes.T, queries, preferred_element_type=jnp.float32)
    query_grad = jnp.dot(slopes, span_low, preferred_element_type=jnp.float32).astype(jnp.bfloat16)
    return (tail_grad, query_grad)


def head_update(head_tab, head_st, rows_h, relation_rows, query_grad):
    edge_grad = conj_product(query_grad.astype(jnp.float32), relation_rows)
    row_ids = jnp.arange(head_tab.shape[0], dtype=jnp.int32)
    selector = (row_ids[:, None] == rows_h[None, :]).astype(jnp.float32)
    head_part = jnp.dot(
        selector, edge_grad, precision=lax.Precision.HIGHEST, preferred_element_type=jnp.float32
    )
    total_grad = lax.psum(head_part.astype(jnp.bfloat16), "narrow").astype(jnp.float32)
    return adagrad(head_tab, head_st, total_grad)


def make_queries(head_tab, relations, rows_h, rows_r):
    relation_rows = jnp.take(relations, rows_r, axis=0).astype(jnp.float32)
    queries = complex_product(jnp.take(head_tab, rows_h, axis=0), relation_rows).astype(
        jnp.bfloat16
    )
    return (queries, relation_rows)


def local(
    head_table, head_state, tail_table, tail_state, relations, head_rows, tail_rows, relation_ids
):
    queries, relation_rows = make_queries(head_table, relations, head_rows[0], relation_ids[0])
    tail_grad, query_grad = edge_terms(queries, tail_table, tail_rows[0])
    tail_tab, tail_st = adagrad(tail_table, tail_state, tail_grad)
    head_tab, head_st = head_update(head_table, head_state, head_rows[0], relation_rows, query_grad)
    queries, relation_rows = make_queries(head_tab, relations, head_rows[1], relation_ids[1])
    moved_tab, moved_st = (
        passed_along(tail_tab.astype(jnp.bfloat16), "wide", 1).astype(tail_tab.dtype),
        passed_along(tail_st.astype(jnp.bfloat16), "wide", 1).astype(tail_st.dtype),
    )
    tail_grad, query_grad = edge_terms(queries, moved_tab, tail_rows[1])
    moved_tab, moved_st = adagrad(moved_tab, moved_st, tail_grad)
    tail_tab, tail_st = (
        passed_along(moved_tab.astype(jnp.bfloat16), "wide", -1).astype(moved_tab.dtype),
        passed_along(moved_st.astype(jnp.bfloat16), "wide", -1).astype(moved_st.dtype),
    )
    head_tab, head_st = head_update(head_tab, head_st, head_rows[1], relation_rows, query_grad)
    return (head_tab, head_st, tail_tab, tail_st)


def solution(mesh):
    return jax.shard_map(
        local,
        mesh=mesh,
        in_specs=(
            P("wide", None),
            P("wide"),
            P(("wide", "narrow"), None),
            P(("wide", "narrow")),
            P(),
            P(None, ("wide", "narrow")),
            P(None, ("wide", "narrow")),
            P(None, ("wide", "narrow")),
        ),
        out_specs=(P("wide", None), P("wide"), P(("wide", "narrow"), None), P(("wide", "narrow"))),
        check_vma=False,
    )
```

profile of v0, /device:TPU:32, one launch (start us, length us, event | category | flops | bytes accessed | tf_op | source)
XLA Modules:
  0.0 245.0 jit_solution(9804627899040501699)
XLA Ops:
  7.2 0.8 fusion.47
  8.0 0.8 fusion.46
  8.8 0.8 fusion.48
  9.6 1.8 copy.12
  11.5 4.9 %gather_fusion = f32[1024,400]{1,0:T(8,128)} fusion(f32[1024,400]{1,0:T(8,128)S(1)} %copy.12, s32[1024]{0:T(1024)S(1)} %fusion.30), kind=kCustom, calls=%fused_computation.clone | custom fusion | bytes 3280896 | tf_op jit(solution)/shard_map/jit(_take)/gather | solution.py:71
  16.4 1.8 copy.13
  18.2 9.6 %copy.14 = bf16[7424,400]{1,0:T(8,128)(2,1)} copy(bf16[7424,400]{0,1:T(8,128)(2,1)} %param.16) | data formatting | bytes 11878400 | tf_op args[4]
  27.8 8.1 %gather_fusion.1 = bf16[1024,400]{1,0:T(8,128)(2,1)S(1)} fusion(bf16[7424,400]{1,0:T(8,128)(2,1)} %copy.14, s32[1024]{0:T(1024)S(1)} %fusion.31), kind=kCustom, calls=%fused_computation.1.clone | custom fusion | bytes 1642496 | tf_op jit(solution)/shard_map/jit(_take)/gather | solution.py:70
  37.1 0.7 copy-done.3
  37.8 1.8 subtract_convert_fusion.1
  39.7 0.6 multiply_reduce_fusion.1
  40.6 2.1 collective-permute-start
  42.7 0.6 fusion.23
  43.8 3.9 %fusion.19 = bf16[1024,400]{0,1:T(8,128)(2,1)} fusion(f32[1024,200]{0,1:T(8,128)S(1)} %get-tuple-element.13, f32[1024,200]{0,1:T(8,128)S(1)} %get-tuple-element.12, s32[1024]{0:T(1024)S(1)} %bitcast.19), kind=kOutput, calls=%fused_computation.31 | convolution fusion | flops 5035032576 | bytes 2461696 | tf_op jit(solution)/shard_map/dot_general | solution.py:62
  48.0 8.1 %gather_fusion.3 = bf16[1024,400]{1,0:T(8,128)(2,1)S(1)} fusion(bf16[7424,400]{1,0:T(8,128)(2,1)} %copy.14, s32[1024]{0:T(1024)S(1)} %fusion.33), kind=kCustom, calls=%fused_computation.3.clone | custom fusion | bytes 1642496 | tf_op jit(solution)/shard_map/jit(_take)/gather | solution.py:70
  56.7 1.3 select_convert_fusion
  58.0 72.9 %all-reduce.3.cloned.1.call-done = bf16[1024,400]{0,1:T(8,128)(2,1)} async-done(((bf16[1024,400]{0,1:T(8,128)(2,1)}), bf16[1024,400]{0,1:T(8,128)(2,1)}) %all-reduce.3.cloned.1.call-update) | async-done | bytes 819216 | tf_op jit(solution)/shard_map/psum | solution.py:65
  130.9 1.3 fusion.6
  132.3 2.6 %fusion.5 = f32[1024,400]{0,1:T(8,128)} fusion(f32[1024,400]{0,1:T(8,128)S(1)} %copy-done.2, bf16[1024,400]{0,1:T(8,128)(2,1)} %all-reduce.3.cloned.1.call-done, f32[1024]{0:T(1024)S(1)} %fusion.34), kind=kLoop, calls=%fused_computation.19 | loop fusion | flops 1638400 | bytes 4100096 | tf_op jit(solution)/shard_map/sub | solution.py:43
  134.9 1.8 copy.16
  136.7 4.9 %gather_fusion.2 = f32[1024,400]{1,0:T(8,128)} fusion(f32[1024,400]{1,0:T(8,128)S(1)} %copy.16, s32[1024]{0:T(1024)S(1)} %fusion.32), kind=kCustom, calls=%fused_computation.2.clone | custom fusion | bytes 3280896 | tf_op jit(solution)/shard_map/jit(_take)/gather | solution.py:71
  141.6 1.8 copy.17
  143.6 1.3 copy-done.1
  145.3 1.8 subtract_convert_fusion
  147.2 0.6 multiply_reduce_fusion
  147.8 0.6 fusion.22
  148.9 3.9 %fusion.16 = bf16[1024,400]{0,1:T(8,128)(2,1)} fusion(f32[1024,200]{0,1:T(8,128)S(1)} %get-tuple-element.9, f32[1024,200]{0,1:T(8,128)S(1)} %get-tuple-element.8, s32[1024]{0:T(1024)S(1)} %bitcast.14), kind=kOutput, calls=%fused_computation.30 | convolution fusion | flops 5035032576 | bytes 2461696 | tf_op jit(solution)/shard_map/dot_general | solution.py:62
  153.7 4.9 %collective-permute-done.3 = bf16[512]{0:T(512)(128)(2,1)S(1)} collective-permute-done((bf16[512]{0:T(512)(128)(2,1)S(1)}, bf16[512]{0:T(512)(128)(2,1)S(1)}, u32[]{:S(2)}, u32[]{:S(2)}) %collective-permute-start.3) | collective-permute-done | bytes 1056 | tf_op jit(solution)/shard_map/ppermute | solution.py:12
  159.2 1.0 convert_element_type.86
  160.2 73.5 %all-reduce.5.cloned.1.call-done = bf16[1024,400]{0,1:T(8,128)(2,1)} async-done(((bf16[1024,400]{0,1:T(8,128)(2,1)}), bf16[1024,400]{0,1:T(8,128)(2,1)}) %all-reduce.5.cloned.1.call-update) | async-done | bytes 819216 | tf_op jit(solution)/shard_map/psum | solution.py:65
  233.7 1.3 fusion.9
  235.6 2.6 %fusion.8 = f32[1024,400]{0,1:T(8,128)} fusion(f32[1024,400]{0,1:T(8,128)S(1)} %copy-done, bf16[1024,400]{0,1:T(8,128)(2,1)} %all-reduce.5.cloned.1.call-done, f32[1024]{0:T(1024)S(1)} %get-tuple-element.6), kind=kLoop, calls=%fused_computation.22 | loop fusion | flops 1638400 | bytes 4100096 | tf_op jit(solution)/shard_map/sub | solution.py:43
  (44 shorter events, 5.8 us)
Async XLA Ops:
  7.2 123.7 %all-reduce.3.cloned.1.call-start = ((), (), s32[]{:S(2)}) async-start(), calls=%async_computation | async-start | bytes 1638400 | tf_op jit(solution)/shard_map/psum | solution.py:65
  36.7 1.1 copy-start.3
  39.7 0.7 copy-start.5
  40.4 112.5 %collective-permute-start.1 = (bf16[512]{0:T(512)(128)(2,1)S(1)}, bf16[512]{0:T(512)(128)(2,1)S(1)}, u32[]{:S(2)}, u32[]{:S(2)}) collective-permute-start(bf16[512]{0:T(512)(128)(2,1)S(1)} %get-tuple-element.22), channel_id=1, source_target_pairs={{0,8},{8,16},{16,24},{24,32},{32,40},{40,48},{48,56},{56,64},{64,7... | collective-permute-start | bytes 3080 | tf_op jit(solution)/shard_map/ppermute | solution.py:12
  40.6 104.7 %collective-permute-start = (bf16[512,400]{0,1:T(8,128)(2,1)S(1)}, bf16[512,400]{0,1:T(8,128)(2,1)S(1)}, u32[]{:S(2)}, u32[]{:S(2)}) collective-permute-start(bf16[512,400]{0,1:T(8,128)(2,1)S(1)} %subtract_convert_fusion.3), channel_id=1, source_target_pairs={{0,8},{8,16},{16,24},{24,32},{32,40},{40,48},{48,56},{56,64},{64,7... | collective-permute-start | bytes 1228808 | tf_op jit(solution)/shard_map/ppermute | solution.py:12
  47.7 185.9 %all-reduce.5.cloned.1.call-start = ((), (), s32[]{:S(2)}) async-start(), calls=%async_computation.1 | async-start | bytes 1638400 | tf_op jit(solution)/shard_map/psum | solution.py:65
  56.7 75.6 %copy-start.4 = (f32[1024]{0:T(1024)S(1)}, f32[1024]{0:T(1024)}, u32[]{:S(2)}) copy-start(f32[1024]{0:T(1024)} %param.13) | copy-start | bytes 12292
  56.7 75.6 %copy-start.2 = (f32[1024,400]{0,1:T(8,128)S(1)}, f32[1024,400]{0,1:T(8,128)}, u32[]{:S(2)}) copy-start(f32[1024,400]{0,1:T(8,128)} %param.12) | copy-start | bytes 4915204
  143.5 1.4 copy-start.1
  152.9 82.8 %copy-start = (f32[1024,400]{0,1:T(8,128)S(1)}, f32[1024,400]{0,1:T(8,128)}, u32[]{:S(2)}) copy-start(f32[1024,400]{0,1:T(8,128)} %fusion.5) | copy-start | bytes 4915204
  153.0 6.2 %collective-permute-start.2 = (bf16[512,400]{0,1:T(8,128)(2,1)S(1)}, bf16[512,400]{0,1:T(8,128)(2,1)S(1)}, u32[]{:S(2)}, u32[]{:S(2)}) collective-permute-start(bf16[512,400]{0,1:T(8,128)(2,1)S(1)} %subtract_convert_fusion.2), channel_id=1, source_target_pairs={{0,248},{8,0},{16,8},{24,16},{32,24},{40,32},{48,40},{56,48},{64,5... | collective-permute-start | bytes 1228808 | tf_op jit(solution)/shard_map/ppermute | solution.py:12
  153.1 5.5 %collective-permute-start.3 = (bf16[512]{0:T(512)(128)(2,1)S(1)}, bf16[512]{0:T(512)(128)(2,1)S(1)}, u32[]{:S(2)}, u32[]{:S(2)}) collective-permute-start(bf16[512]{0:T(512)(128)(2,1)S(1)} %get-tuple-element.24), channel_id=1, source_target_pairs={{0,248},{8,0},{16,8},{24,16},{32,24},{40,32},{48,40},{56,48},{64,5... | collective-permute-start | bytes 3080 | tf_op jit(solution)/shard_map/ppermute | solution.py:12
Sparse Core Ops, SparseCore 0:
  47.9 82.9 all-reduce.2
  152.9 80.6 all-reduce.4
where the time goes:
time: 246 us; the launch traced here: 245 us
  waiting for transfers between devices  151 us (61%)
  local copies, waits for them, and re-layouts  48.4 us (20%)
  between operations  14.4 us (6%)
  matrix products  13.9 us (6%)
  other arithmetic  13.8 us (6%)
  starting transfers between devices  3.08 us (1%)
    psum x2, waiting for transfers between devices, head_update(): lax.psum(head_part.astype(jnp.bfloat16), 'narrow').astype(jnp.float32)  146 us
    gather x4, local copies, waits for them, and re-layouts, make_queries(): relation_rows = jnp.take(relations, rows_r, axis=0).astype(jnp.float32)  17.2 us
    unnamed x14, local copies, waits for them, and re-layouts  13.5 us
    gather x4, local copies, waits for them, and re-layouts, make_queries(): jnp.take(head_tab, rows_h, axis=0)  13.5 us
    dot_general x2, matrix products, head_update(): jnp.dot(selector, edge_grad, precision=lax.Precision.HIGHEST, preferred_e...  7.83 us
    sub x2, other arithmetic, adagrad(): return (table - learning * grad / jnp.sqrt(state_new)[:, None], state_new)  5.18 us
  transfers between devices with their start and end apart: 6, of which 3 were waited for; matrix products, arithmetic and copies ran while one was open for 15% of the time, Pallas kernels for 0%

commit v1 on v0

v1 whole, which is shorter than its diff:
```python
import functools

import jax
import jax.numpy as jnp
from jax import lax
from jax.experimental import pallas as pl
from jax.experimental.pallas import tpu as pltpu
from jax.sharding import PartitionSpec as P

learning = 0.1
BF = jnp.bfloat16
F32 = jnp.float32
VMEM = pl.BlockSpec(memory_space=pltpu.VMEM)
ANY = pl.BlockSpec(memory_space=pl.ANY)
LIMIT = 48 * 1024 * 1024


def call(kernel, outs, ins, scratch=(), flops=0, nbytes=0):
    return pl.pallas_call(
        kernel,
        out_shape=[jax.ShapeDtypeStruct(s, d) for s, d in outs],
        in_specs=ins,
        out_specs=[VMEM] * len(outs),
        scratch_shapes=list(scratch),
        compiler_params=pltpu.CompilerParams(vmem_limit_bytes=LIMIT),
        cost_estimate=pl.CostEstimate(flops=flops, bytes_accessed=nbytes, transcendentals=0),
    )


def one_hot(idx, first, count):
    rows = lax.broadcasted_iota(jnp.int32, (count, idx.shape[1]), 0)
    return jnp.where(rows == idx - first, 1.0, 0.0).astype(BF)


def dot(a, b, dims=((1,), (0,))):
    return lax.dot_general(a, b, (dims, ((), ())), preferred_element_type=F32)


def relation_kernel(bucket, chunk, ids_ref, rel_hbm, out_ref, rel_ref, acc_ref, sem):
    count = rel_hbm.shape[1] // chunk

    def copy(c):
        cols = pl.ds(pl.multiple_of(c * chunk, chunk), chunk)
        return pltpu.make_async_copy(rel_hbm.at[:, cols], rel_ref.at[:, cols], sem.at[c])

    def begin(c, _):
        copy(c).start()
        return 0

    lax.fori_loop(0, count, begin, 0)
    ids = ids_ref[bucket : bucket + 1, :]
    acc_ref[...] = jnp.zeros_like(acc_ref)

    def step(c, _):
        copy(c).wait()
        cols = pl.ds(pl.multiple_of(c * chunk, chunk), chunk)
        acc_ref[...] += dot(rel_ref[:, cols], one_hot(ids, c * chunk, chunk))
        return 0

    lax.fori_loop(0, count, step, 0)
    out_ref[...] = acc_ref[...].astype(BF)


def gather_relations(bucket, ids, rel_t):
    chunk = 256
    depth, types = rel_t.shape
    edges = ids.shape[1]
    return call(
        functools.partial(relation_kernel, bucket, chunk),
        [((depth, edges), BF)],
        [VMEM, ANY],
        [
            pltpu.VMEM((depth, types), BF),
            pltpu.VMEM((depth, edges), F32),
            pltpu.SemaphoreType.DMA((types // chunk,)),
        ],
        flops=2 * depth * types * edges,
        nbytes=2 * depth * types,
    )(ids, rel_t)[0]


def edge_work(bucket, head, span_low, rel_ref, rows_ref, tails_ref, part_ref, q_ref, sl_ref, hot_ref):
    half = head.shape[0] // 2
    hrows = head.shape[1]
    trows = span_low.shape[1]
    hot_ref[...] = one_hot(rows_ref[bucket : bucket + 1, :], 0, hrows)
    high = head.astype(BF)
    low = (head - high.astype(F32)).astype(BF)
    h = dot(high, hot_ref[...]) + dot(low, hot_ref[...])
    r = rel_ref[...].astype(F32)
    h_re, h_im, r_re, r_im = h[:half], h[half:], r[:half], r[half:]
    q_ref[...] = jnp.concatenate(
        [h_re * r_re - h_im * r_im, h_re * r_im + h_im * r_re], axis=0
    ).astype(BF)
    scores = dot(span_low, q_ref[...], ((0,), (0,)))
    soft = jnp.tanh(0.5 * scores) * 0.5 + 0.5
    at = lax.broadcasted_iota(jnp.int32, scores.shape, 0) == tails_ref[bucket : bucket + 1, :]
    sl_ref[...] = jnp.where(at, soft * (1.0 / trows) - (1.0 - soft), soft * (1.0 / trows)).astype(BF)
    g = dot(span_low, sl_ref[...])
    g_re, g_im = g[:half], g[half:]
    edge = jnp.concatenate(
        [g_re * r_re + g_im * r_im, g_im * r_re - g_re * r_im], axis=0
    ).astype(BF)
    part = dot(edge, hot_ref[...], ((1,), (1,))).astype(BF)
    width = part_ref.shape[2]
    for n in range(part_ref.shape[0]):
        part_ref[n] = part[:, n * width : (n + 1) * width]


def first_kernel(head_ref, tail_ref, rel_ref, rows_ref, tails_ref, part_ref, q_ref, sl_ref, hot_ref):
    edge_work(
        0, head_ref[...], tail_ref[...].astype(BF), rel_ref, rows_ref, tails_ref, part_ref, q_ref, sl_ref, hot_ref
    )


def stepped(table, state, grad):
    state_new = state + jnp.sum(grad * grad, axis=0, keepdims=True) * (1.0 / grad.shape[0])
    return table - (learning * lax.rsqrt(state_new)) * grad, state_new


def joined(sums_ref):
    return jnp.concatenate([sums_ref[n] for n in range(sums_ref.shape[0])], axis=1).astype(F32)


def second_kernel(
    head_ref, state_ref, sums_ref, span_ref, rel_ref, rows_ref, tails_ref,
    part_ref, q_ref, sl_ref, head_out, state_out, hot_ref,
):
    head, state = stepped(head_ref[...], state_ref[...], joined(sums_ref))
    head_out[...] = head
    state_out[...] = state
    edge_work(1, head, span_ref[...], rel_ref, rows_ref, tails_ref, part_ref, q_ref, sl_ref, hot_ref)


def tail_kernel(q_ref, sl_ref, tail_ref, state_ref, tail_out, state_out, low_out):
    grad = dot(q_ref[...], sl_ref[...], ((1,), (1,)))
    tail, state = stepped(tail_ref[...], state_ref[...], grad)
    tail_out[...] = tail
    state_out[...] = state
    low_out[...] = tail.astype(BF)


def grad_kernel(q_ref, sl_ref, grad_out):
    grad_out[...] = dot(q_ref[...], sl_ref[...], ((1,), (1,))).astype(BF)


def tail_end_kernel(tail_ref, state_ref, grad_ref, tail_out, state_out):
    tail_out[...], state_out[...] = stepped(tail_ref[...], state_ref[...], grad_ref[...].astype(F32))


def head_end_kernel(head_ref, state_ref, sums_ref, head_out, state_out):
    head_out[...], state_out[...] = stepped(head_ref[...], state_ref[...], joined(sums_ref))


def passed_along(value, axis, steps):
    count = lax.axis_size(axis)
    return lax.ppermute(value, axis, [(source, (source + steps) % count) for source in range(count)])


def summed(part):
    got = lax.all_to_all(part, "narrow", 0, 0, tiled=True)
    mine = jnp.sum(got.astype(F32), axis=0).astype(BF)
    return lax.all_to_all(jnp.broadcast_to(mine[None], part.shape), "narrow", 0, 0, tiled=True)


def local(head_table, head_state, tail_table, tail_state, relations, head_rows, tail_rows, relation_ids):
    head, tail, rel = head_table.T, tail_table.T, relations.T
    h_state, t_state = head_state[None], tail_state[None]
    depth, hrows = head.shape
    trows = tail.shape[1]
    edges = head_rows.shape[1]
    groups = lax.axis_size("narrow")
    edge_outs = [((groups, depth, hrows // groups), BF), ((depth, edges), BF), ((trows, edges), BF)]
    hot = [pltpu.VMEM((hrows, edges), BF)]
    edge_flops = 2 * depth * edges * (2 * trows + 3 * hrows)

    rel_0 = gather_relations(0, relation_ids, rel)
    part, q, slopes = call(first_kernel, edge_outs, [VMEM] * 5, hot, edge_flops, 8 << 20)(
        head, tail, rel_0, head_rows, tail_rows
    )
    tail, t_state, low = call(
        tail_kernel, [((depth, trows), F32), ((1, trows), F32), ((depth, trows), BF)], [VMEM] * 4,
        (), 2 * depth * edges * trows, 4 << 20,
    )(q, slopes, tail, t_state)
    rel_1 = gather_relations(1, relation_ids, rel)
    low = passed_along(low, "wide", 1)
    sums = summed(part)
    part, q, slopes, head, h_state = call(
        second_kernel, edge_outs + [((depth, hrows), F32), ((1, hrows), F32)], [VMEM] * 7, hot, edge_flops, 9 << 20
    )(head, h_state, sums, low, rel_1, head_rows, tail_rows)
    grad = call(grad_kernel, [((depth, trows), BF)], [VMEM] * 2, (), 2 * depth * edges * trows, 2 << 20)(q, slopes)[0]
    grad = passed_along(grad, "wide", -1)
    sums = summed(part)
    tail, t_state = call(
        tail_end_kernel, [((depth, trows), F32), ((1, trows), F32)], [VMEM] * 3, (), 0, 2 << 20
    )(tail, t_state, grad)
    head, h_state = call(
        head_end_kernel, [((depth, hrows), F32), ((1, hrows), F32)], [VMEM] * 3, (), 0, 4 << 20
    )(head, h_state, sums)
    return head.T, h_state[0], tail.T, t_state[0]


def solution(mesh):
    return jax.shard_map(
        local,
        mesh=mesh,
        in_specs=(
            P("wide", None),
            P("wide"),
            P(("wide", "narrow"), None),
            P(("wide", "narrow")),
            P(),
            P(None, ("wide", "narrow")),
            P(None, ("wide", "narrow")),
            P(None, ("wide", "narrow")),
        ),
        out_specs=(P("wide", None), P("wide"), P(("wide", "narrow"), None), P(("wide", "narrow"))),
        check_vma=False,
    )
```

time: 246 us -> 111 us (0.45)
  the two profiles are of different devices: /device:TPU:32 before, /device:TPU:1 now
where the time goes in v1:
time: 111 us
  Pallas kernels  42.8 us (39%)
  blocking collectives  35.9 us (32%)
  waiting for transfers between devices  11.1 us (10%)
  starting transfers between devices  10.9 us (10%)
  local copies, waits for them, and re-layouts  8.68 us (8%)
    all_to_all x2, blocking collectives, summed(): got = lax.all_to_all(part, 'narrow', 0, 0, tiled=True)  35.9 us
    pallas_call x2, Pallas kernels, gather_relations(): call(functools.partial(relation_kernel, bucket, chunk), [((depth, edges),...  27.9 us
    ppermute x2, waiting for transfers between devices, passed_along(): lax.ppermute(value, axis, [(source, (source + steps) % count) for source...  7.66 us
    all_to_all x2, starting transfers between devices, summed(): lax.all_to_all(jnp.broadcast_to(mine[None], part.shape), 'narrow', 0, 0,...  7.1 us
    pallas_call x1, Pallas kernels, local(): call(second_kernel, edge_outs + [((depth, hrows), F32), ((1, hrows), F32)...  6.29 us
    unnamed x30, local copies, waits for them, and re-layouts  5.78 us
    pallas_call x1, Pallas kernels, local(): call(first_kernel, edge_outs, [VMEM] * 5, hot, edge_flops, 8 << 20)  4.39 us
    ppermute x2, starting transfers between devices, passed_along(): lax.ppermute(value, axis, [(source, (source + steps) % count) for source...  3.78 us
  transfers between devices with their start and end apart: 4, of which 2 were waited for; matrix products, arithmetic and copies ran while one was open for 0% of the time, Pallas kernels for 15%

profile of v1, /device:TPU:1, one launch (start us, length us, event | category | flops | bytes accessed | tf_op | source)
XLA Modules:
  0.0 111.0 jit_solution(10841678667689349722)
XLA Ops:
  0.6 0.0 copy-start.10
  0.6 0.7 copy-done.10
  1.3 14.0 %shard_map.111.rel_ref = bf16[400,1024]{1,0:T(8,128)(2,1)S(1)} custom-call(s32[2,1024]{1,0:T(2,128)S(1)} %copy-done.10, bf16[400,7424]{1,0:T(8,128)(2,1)} %bitcast.15), custom_call_target="tpu_custom_call" | custom-call | flops 6081740800 | bytes 5939200 | tf_op jit(solution)/shard_map/pallas_call | solution.py:68
  15.4 4.4 %shard_map.112 = (bf16[8,400,128]{2,1,0:T(8,128)(2,1)S(1)}, bf16[400,1024]{1,0:T(8,128)(2,1)S(1)}, bf16[512,1024]{1,0:T(8,128)(2,1)S(1)}) custom-call(f32[400,1024]{1,0:T(8,128)S(1)} %bitcast.13, f32[400,512]{1,0:T(8,128)S(1)} %bitcast.9, bf16[400,1024]{1,0:T(8,128)(2,1)S(1)} %shard_map.111.rel_ref, s32[2,1024]{1,0:T(2,128)S(1)} %copy-done.12, ...), custom_call_target="tpu_custom_call" | custom-call | flops 3355443200 | bytes 8388608 | tf_op jit(solution)/shard_map/pallas_call | solution.py:178
  19.8 17.9 %all_to_all.20 = bf16[8,400,128]{2,1,0:T(8,128)(2,1)S(1)} all-to-all(bf16[8,400,128]{2,1,0:T(8,128)(2,1)S(1)} %get-tuple-element.19), channel_id=1, replica_groups=mesh['wide'=32,'narrow'=8] {'narrow'}, dimensions={0} | all-to-all | bytes 1638400 | tf_op jit(solution)/shard_map/all_to_all | solution.py:161
  37.7 0.8 reduce_sum.24
  38.4 1.9 %broadcast_in_dim.9 = bf16[8,400,128]{2,1,0:T(8,128)(2,1)} broadcast(bf16[400,128]{1,0:T(8,128)(2,1)} %reduce_sum.24), dimensions={1,2} | broadcast | bytes 921600 | tf_op jit(solution)/shard_map/broadcast_in_dim | solution.py:163
  40.3 3.5 %all-to-all-start.1 = ((bf16[8,400,128]{2,1,0:T(8,128)(2,1)}), bf16[8,400,128]{2,1,0:T(8,128)(2,1)S(1)}, u32[]{:S(2)}, u32[]{:S(2)}) async-start(bf16[8,400,128]{2,1,0:T(8,128)(2,1)} %broadcast_in_dim.9), calls=%async_computation.1 | async-start | bytes 1638400 | tf_op jit(solution)/shard_map/all_to_all | solution.py:163
  43.9 0.0 copy-start.11
  43.9 0.8 shard_map.113
  44.7 0.9 copy-done.2
  45.7 3.7 %collective-permute-start = (bf16[400,512]{1,0:T(8,128)(2,1)S(1)}, bf16[400,512]{1,0:T(8,128)(2,1)S(1)}, u32[]{:S(2)}, u32[]{:S(2)}) collective-permute-start(bf16[400,512]{1,0:T(8,128)(2,1)S(1)} %get-tuple-element.22), channel_id=1, source_target_pairs={{0,8},{8,16},{16,24},{24,32},{32,40},{40,48},{48,56},{56,64},{64,7... | collective-permute-start | bytes 1228808 | tf_op jit(solution)/shard_map/ppermute | solution.py:157
  49.4 13.9 %shard_map.114.rel_ref = bf16[400,1024]{1,0:T(8,128)(2,1)S(1)} custom-call(s32[2,1024]{1,0:T(2,128)S(1)} %copy-done.11, bf16[400,7424]{1,0:T(8,128)(2,1)} %bitcast.16), custom_call_target="tpu_custom_call" | custom-call | flops 6081740800 | bytes 5939200 | tf_op jit(solution)/shard_map/pallas_call | solution.py:68
  63.2 0.0 collective-permute-done.span_ref
  63.3 0.0 copy-start.4
  63.3 0.9 copy-done.4
  64.2 1.1 %copy-done.5 = bf16[8,400,128]{2,1,0:T(8,128)(2,1)S(1)} copy-done((bf16[8,400,128]{2,1,0:T(8,128)(2,1)S(1)}, bf16[8,400,128]{2,1,0:T(8,128)(2,1)}, u32[]{:S(2)}) %copy-start.5) | copy-done | bytes 819224
  65.3 6.3 %shard_map.115 = (bf16[8,400,128]{2,1,0:T(8,128)(2,1)S(1)}, bf16[400,1024]{1,0:T(8,128)(2,1)S(1)}, bf16[512,1024]{1,0:T(8,128)(2,1)S(1)}, f32[400,1024]{1,0:T(8,128)}, f32[1,1024]{1,0:T(1,128)S(1)}) custom-call(f32[400,1024]{1,0:T(8,128)} %bitcast.12, f32[1,1024]{1,0:T(1,128)S(1)} %bitcast.14, bf16[8,400,128]{2,1,0:T(8,128)(2,1)S(1)} %copy-done.5, ...), custom_call_target="tpu_custom_call" | custom-call | flops 3355443200 | bytes 9437184 | tf_op jit(solution)/shard_map/pallas_call | solution.py:188
  71.6 0.0 copy-start.6
  71.6 0.9 copy-done.6
  72.5 18.0 %all_to_all.21 = bf16[8,400,128]{2,1,0:T(8,128)(2,1)S(1)} all-to-all(bf16[8,400,128]{2,1,0:T(8,128)(2,1)S(1)} %get-tuple-element.25), channel_id=1, replica_groups=mesh['wide'=32,'narrow'=8] {'narrow'}, dimensions={0} | all-to-all | bytes 1638400 | tf_op jit(solution)/shard_map/all_to_all | solution.py:161
  90.5 0.1 reduce_sum.25
  90.6 1.0 broadcast_in_dim.21
  91.6 3.5 %all-to-all-start.3 = ((bf16[8,400,128]{2,1,0:T(8,128)(2,1)}), bf16[8,400,128]{2,1,0:T(8,128)(2,1)S(1)}, u32[]{:S(2)}, u32[]{:S(2)}) async-start(bf16[8,400,128]{2,1,0:T(8,128)(2,1)} %broadcast_in_dim.21), calls=%async_computation.3 | async-start | bytes 1638400 | tf_op jit(solution)/shard_map/all_to_all | solution.py:163
  95.2 0.0 copy-start.7
  95.2 1.2 %copy-done.7 = bf16[400,1024]{1,0:T(8,128)(2,1)S(1)} copy-done((bf16[400,1024]{1,0:T(8,128)(2,1)S(1)}, bf16[400,1024]{1,0:T(8,128)(2,1)}, u32[]{:S(2)}) %copy-start.7) | copy-done | bytes 819224
  96.4 0.6 shard_map.117
  97.0 0.1 collective-permute-start.1
  97.1 7.7 %collective-permute-done.1.grad_ref = bf16[400,512]{1,0:T(8,128)(2,1)S(1)} collective-permute-done((bf16[400,512]{1,0:T(8,128)(2,1)S(1)}, bf16[400,512]{1,0:T(8,128)(2,1)S(1)}, u32[]{:S(2)}, u32[]{:S(2)}) %collective-permute-start.1) | collective-permute-done | bytes 409632 | tf_op jit(solution)/shard_map/ppermute | solution.py:157
  104.8 1.1 shard_map.118
  105.9 3.4 %all-to-all-done.3.sums_ref = bf16[8,400,128]{2,1,0:T(8,128)(2,1)S(1)} async-done(((bf16[8,400,128]{2,1,0:T(8,128)(2,1)}), bf16[8,400,128]{2,1,0:T(8,128)(2,1)S(1)}, u32[]{:S(2)}, u32[]{:S(2)}) %all-to-all-start.3) | async-done | bytes 819232 | tf_op jit(solution)/shard_map/all_to_all | solution.py:163
  109.3 1.7 %shard_map.116 = (f32[400,1024]{1,0:T(8,128)}, f32[1,1024]{1,0:T(1,128)}) custom-call(f32[400,1024]{1,0:T(8,128)S(1)} %copy-done, f32[1,1024]{1,0:T(1,128)S(1)} %get-tuple-element.24.state_ref, bf16[8,400,128]{2,1,0:T(8,128)(2,1)S(1)} %all-to-all-done.3.sums_ref), custom_call_target="tpu_custom_call" | custom-call | bytes 4194304 | tf_op jit(solution)/shard_map/pallas_call | solution.py:197
  (20 shorter events, 0.0 us)
Async XLA Ops:
  0.6 0.7 copy-start.10
  1.3 14.0 %copy-start.1 = (f32[512,400]{0,1:T(8,128)S(1)}, f32[512,400]{0,1:T(8,128)}, u32[]{:S(2)}) copy-start(f32[512,400]{0,1:T(8,128)} %param.10) | copy-start | bytes 2457604
  1.3 14.0 %copy-start.9 = (f32[1024,400]{0,1:T(8,128)S(1)}, f32[1024,400]{0,1:T(8,128)}, u32[]{:S(2)}) copy-start(f32[1024,400]{0,1:T(8,128)} %param.8) | copy-start | bytes 4915204
  1.3 14.0 %copy-start.12 = (s32[2,1024]{1,0:T(2,128)S(1)}, s32[2,1024]{1,0:T(2,128)}, u32[]{:S(2)}) copy-start(s32[2,1024]{1,0:T(2,128)} %rows_ref.3) | copy-start | bytes 24580
  1.3 14.0 %copy-start.13 = (s32[2,1024]{1,0:T(2,128)S(1)}, s32[2,1024]{1,0:T(2,128)}, u32[]{:S(2)}) copy-start(s32[2,1024]{1,0:T(2,128)} %tails_ref.3) | copy-start | bytes 24580
  37.7 6.2 %copy-start.8 = (f32[512]{0:T(512)S(1)}, f32[512]{0:T(512)}, u32[]{:S(2)}) copy-start(f32[512]{0:T(512)} %param.11) | copy-start | bytes 6148
  40.3 22.9 %all-to-all-start.1 = ((bf16[8,400,128]{2,1,0:T(8,128)(2,1)}), bf16[8,400,128]{2,1,0:T(8,128)(2,1)S(1)}, u32[]{:S(2)}, u32[]{:S(2)}) async-start(bf16[8,400,128]{2,1,0:T(8,128)(2,1)} %broadcast_in_dim.9), calls=%async_computation.1 | async-start | bytes 1638400 | tf_op jit(solution)/shard_map/all_to_all | solution.py:163
  43.9 5.5 %copy-start.11 = (s32[2,1024]{1,0:T(2,128)S(1)}, s32[2,1024]{1,0:T(2,128)}, u32[]{:S(2)}) copy-start(s32[2,1024]{1,0:T(2,128)} %ids_ref.3) | copy-start | bytes 24580
  44.7 0.9 copy-start.2
  45.7 18.5 %copy-start.14 = (f32[1024]{0:T(1024)S(1)}, f32[1024]{0:T(1024)}, u32[]{:S(2)}) copy-start(f32[1024]{0:T(1024)} %param.9) | copy-start | bytes 12292
  45.7 17.6 %collective-permute-start = (bf16[400,512]{1,0:T(8,128)(2,1)S(1)}, bf16[400,512]{1,0:T(8,128)(2,1)S(1)}, u32[]{:S(2)}, u32[]{:S(2)}) collective-permute-start(bf16[400,512]{1,0:T(8,128)(2,1)S(1)} %get-tuple-element.22), channel_id=1, source_target_pairs={{0,8},{8,16},{16,24},{24,32},{32,40},{40,48},{48,56},{56,64},{64,7... | collective-permute-start | bytes 1228808 | tf_op jit(solution)/shard_map/ppermute | solution.py:157
  63.3 0.9 copy-start.4
  64.2 1.1 %copy-start.5 = (bf16[8,400,128]{2,1,0:T(8,128)(2,1)S(1)}, bf16[8,400,128]{2,1,0:T(8,128)(2,1)}, u32[]{:S(2)}) copy-start(bf16[8,400,128]{2,1,0:T(8,128)(2,1)} %copy-done.4) | copy-start | bytes 2457604
  71.6 0.9 copy-start.6
  91.6 17.7 %all-to-all-start.3 = ((bf16[8,400,128]{2,1,0:T(8,128)(2,1)}), bf16[8,400,128]{2,1,0:T(8,128)(2,1)S(1)}, u32[]{:S(2)}, u32[]{:S(2)}) async-start(bf16[8,400,128]{2,1,0:T(8,128)(2,1)} %broadcast_in_dim.21), calls=%async_computation.3 | async-start | bytes 1638400 | tf_op jit(solution)/shard_map/all_to_all | solution.py:163
  95.2 9.6 %copy-start.3 = (f32[400,512]{1,0:T(8,128)S(1)}, f32[400,512]{1,0:T(8,128)}, u32[]{:S(2)}) copy-start(f32[400,512]{1,0:T(8,128)} %copy-done.2) | copy-start | bytes 2457604
  95.2 1.2 %copy-start.7 = (bf16[400,1024]{1,0:T(8,128)(2,1)S(1)}, bf16[400,1024]{1,0:T(8,128)(2,1)}, u32[]{:S(2)}) copy-start(bf16[400,1024]{1,0:T(8,128)(2,1)} %copy-done.6) | copy-start | bytes 2457604
  96.4 12.9 %copy-start = (f32[400,1024]{1,0:T(8,128)S(1)}, f32[400,1024]{1,0:T(8,128)}, u32[]{:S(2)}) copy-start(f32[400,1024]{1,0:T(8,128)} %get-tuple-element.23.head_ref) | copy-start | bytes 4915204
  97.0 7.7 %collective-permute-start.1 = (bf16[400,512]{1,0:T(8,128)(2,1)S(1)}, bf16[400,512]{1,0:T(8,128)(2,1)S(1)}, u32[]{:S(2)}, u32[]{:S(2)}) collective-permute-start(bf16[400,512]{1,0:T(8,128)(2,1)S(1)} %shard_map.117), channel_id=1, source_target_pairs={{0,248},{8,0},{16,8},{24,16},{32,24},{40,32},{48,40},{56,48},{64,5... | collective-permute-start | bytes 1228808 | tf_op jit(solution)/shard_map/ppermute | solution.py:157

commit v2 on v1

v2 whole, which is shorter than its diff:
```python
import functools

import jax
import jax.numpy as jnp
from jax import lax
from jax.experimental import pallas as pl
from jax.experimental.pallas import tpu as pltpu
from jax.sharding import PartitionSpec as P

learning = 0.1
BF = jnp.bfloat16
F32 = jnp.float32
VMEM = pl.BlockSpec(memory_space=pltpu.VMEM)
ANY = pl.BlockSpec(memory_space=pl.ANY)
LANES = 128
TILE = 512
PIECES = 8


def call(kernel, outs, ins, scratch=(), mib=32, flops=0, nbytes=0, out_specs=None):
    return pl.pallas_call(
        kernel,
        out_shape=[jax.ShapeDtypeStruct(s, d) for s, d in outs],
        in_specs=ins,
        out_specs=out_specs or [VMEM] * len(outs),
        scratch_shapes=list(scratch),
        compiler_params=pltpu.CompilerParams(vmem_limit_bytes=mib << 20),
        cost_estimate=pl.CostEstimate(flops=flops, bytes_accessed=nbytes, transcendentals=0),
    )


def one_hot(idx, first, count):
    rows = lax.broadcasted_iota(jnp.int32, (count, idx.shape[1]), 0)
    return jnp.where(rows == idx - first, 1.0, 0.0).astype(BF)


def dot(a, b, dims=((1,), (0,))):
    return lax.dot_general(a, b, (dims, ((), ())), preferred_element_type=F32)


def pieces_of(width):
    blocks = width // LANES
    each = -(-blocks // PIECES)
    return [(p * each * LANES, min(each, blocks - p * each) * LANES) for p in range(PIECES)]


def relation_copies(rel_hbm, rel_ref, sem):
    return [
        pltpu.make_async_copy(rel_hbm.at[:, pl.ds(a, n)], rel_ref.at[:, pl.ds(a, n)], sem.at[p])
        for p, (a, n) in enumerate(pieces_of(rel_hbm.shape[1]))
    ]


def relation_tile(rel_ref, ids, copies):
    total = None
    for p, (a, n) in enumerate(pieces_of(rel_ref.shape[1])):
        if copies is not None:
            copies[p].wait()
        term = dot(rel_ref[:, a : a + n], one_hot(ids, a, n))
        total = term if total is None else total + term
    return total


def relation_kernel(bucket, ids_ref, rel_hbm, out_ref, rel_ref, sem):
    copies = relation_copies(rel_hbm, rel_ref, sem)
    for copy in copies:
        copy.start()
    for t in range(ids_ref.shape[1] // TILE):
        cols = pl.ds(t * TILE, TILE)
        out_ref[:, cols] = relation_tile(rel_ref, ids_ref[bucket : bucket + 1, cols], None if t else copies).astype(BF)


def edge_tile(h, r, low, tails):
    half = h.shape[0] // 2
    h_re, h_im, r_re, r_im = h[:half], h[half:], r[:half], r[half:]
    q = jnp.concatenate([h_re * r_re - h_im * r_im, h_re * r_im + h_im * r_re], axis=0).astype(BF)
    t = jnp.tanh(0.5 * dot(low, q, ((0,), (0,))))
    at = lax.broadcasted_iota(jnp.int32, t.shape, 0) == tails
    k = 0.5 / low.shape[1]
    slopes = jnp.where(at, t * (k + 0.5) + (k - 0.5), t * k + k).astype(BF)
    g = dot(low, slopes)
    g_re, g_im = g[:half], g[half:]
    edge = jnp.concatenate([g_re * r_re + g_im * r_im, g_im * r_re - g_re * r_im], axis=0).astype(BF)
    return q, slopes, edge


def scatter(part_ref, edge_ref, hot_ref):
    width = part_ref.shape[2]
    for n in range(part_ref.shape[0]):
        part_ref[n] = dot(edge_ref[...], hot_ref[n * width : (n + 1) * width, :], ((1,), (1,))).astype(BF)


def stepped(table, state, grad):
    state_new = state + jnp.sum(grad * grad, axis=0, keepdims=True) * (1.0 / grad.shape[0])
    return table - (learning * lax.rsqrt(state_new)) * grad, state_new


def first_kernel(
    head_hbm, tail_hbm, rel_hbm, rows_hbm, tails_hbm, ids_hbm, state_ref, part_ref, tail_out, state_out, low_out,
    head_ref, tail_ref, rel_ref, rows_ref, tails_ref, ids_ref, hot_ref, low_ref, h_ref, edge_ref, q_ref, sl_ref, sem, rel_sem,
):
    pairs = [(rows_hbm, rows_ref), (ids_hbm, ids_ref), (head_hbm, head_ref), (tails_hbm, tails_ref), (tail_hbm, tail_ref)]
    copies = [pltpu.make_async_copy(a, b, sem.at[i]) for i, (a, b) in enumerate(pairs)]
    rel_copies = relation_copies(rel_hbm, rel_ref, rel_sem)
    for copy in copies + rel_copies:
        copy.start()
    copies[0].wait()
    hot_ref[...] = one_hot(rows_ref[0:1, :], 0, head_ref.shape[1])
    copies[1].wait()
    copies[2].wait()
    h_ref[...] = dot(head_ref[...].astype(BF), hot_ref[...])
    copies[3].wait()
    copies[4].wait()
    low_ref[...] = tail_ref[...].astype(BF)
    for t in range(ids_ref.shape[1] // TILE):
        cols = pl.ds(t * TILE, TILE)
        r = relation_tile(rel_ref, ids_ref[0:1, cols], None if t else rel_copies)
        q_ref[:, cols], sl_ref[:, cols], edge_ref[:, cols] = edge_tile(
            h_ref[:, cols], r, low_ref[...], tails_ref[0:1, cols]
        )
    scatter(part_ref, edge_ref, hot_ref)
    tail, state_out[...] = stepped(tail_ref[...], state_ref[...], dot(q_ref[...], sl_ref[...], ((1,), (1,))))
    tail_out[...] = tail
    low_out[...] = tail.astype(BF)


def sum_kernel(got_ref, out_ref):
    total = got_ref[0].astype(F32)
    for n in range(1, got_ref.shape[0]):
        total = total + got_ref[n].astype(F32)
    total = total.astype(BF)
    for n in range(out_ref.shape[0]):
        out_ref[n] = total


def second_kernel(
    head_ref, state_ref, sums_ref, low_ref, rel_ref, rows_ref, tails_ref, part_ref, grad_out,
    head_low, hot_ref, edge_ref, q_ref, sl_ref,
):
    groups, _, width = sums_ref.shape
    for n in range(groups):
        cols = pl.ds(n * width, width)
        head_low[:, cols] = stepped(head_ref[:, cols], state_ref[:, cols], sums_ref[n].astype(F32))[0].astype(BF)
    hot_ref[...] = one_hot(rows_ref[1:2, :], 0, head_ref.shape[1])
    for t in range(rows_ref.shape[1] // TILE):
        cols = pl.ds(t * TILE, TILE)
        h = dot(head_low[...], hot_ref[:, cols])
        q_ref[:, cols], sl_ref[:, cols], edge_ref[:, cols] = edge_tile(
            h, rel_ref[:, cols].astype(F32), low_ref[...], tails_ref[1:2, cols]
        )
    scatter(part_ref, edge_ref, hot_ref)
    grad_out[...] = dot(q_ref[...], sl_ref[...], ((1,), (1,))).astype(BF)


def tail_end_kernel(tail_ref, state_ref, grad_ref, tail_out, state_out):
    tail_out[...], state_out[...] = stepped(tail_ref[...], state_ref[...], grad_ref[...].astype(F32))


def head_kernel(head_ref, state_ref, sums_ref, head_out, state_out):
    groups, _, width = sums_ref.shape
    for n in range(groups):
        cols = pl.ds(n * width, width)
        head_out[:, cols], state_out[:, cols] = stepped(
            head_ref[:, cols], state_ref[:, cols], sums_ref[n].astype(F32)
        )


def passed_along(value, axis, steps):
    count = lax.axis_size(axis)
    return lax.ppermute(value, axis, [(source, (source + steps) % count) for source in range(count)])


def spread(got, *before):
    same = call(sum_kernel, [(got.shape, BF)], [VMEM], (), 24, 0, 2 << 20)(got)[0]
    same, *before = lax.optimization_barrier((same, *before))
    return lax.all_to_all(same, "narrow", 0, 0, tiled=True), *before


def local(head_table, head_state, tail_table, tail_state, relations, head_rows, tail_rows, relation_ids):
    head, tail, rel = head_table.T, tail_table.T, relations.T
    h_state, t_state = head_state[None], tail_state[None]
    depth, hrows = head.shape
    types = rel.shape[1]
    trows = tail.shape[1]
    edges = head_rows.shape[1]
    groups = lax.axis_size("narrow")
    width = hrows // groups
    part_out = ((groups, depth, width), BF)
    edge_flops = 2 * depth * edges * (3 * trows + 2 * hrows)
    rel_flops = 2 * depth * types * edges
    ints = pltpu.VMEM(head_rows.shape, jnp.int32)
    hot = pltpu.VMEM((hrows, edges), BF)
    edge = pltpu.VMEM((depth, edges), BF)
    slope = pltpu.VMEM((trows, edges), BF)
    rel_scratch = pltpu.VMEM(rel.shape, BF)
    rel_sem = pltpu.SemaphoreType.DMA((PIECES,))

    part, tail, t_state, low = call(
        first_kernel, [part_out, (tail.shape, F32), ((1, trows), F32), (tail.shape, BF)], [ANY] * 6 + [VMEM],
        [
            pltpu.VMEM(head.shape, F32), pltpu.VMEM(tail.shape, F32), rel_scratch, ints, ints, ints,
            hot, pltpu.VMEM(tail.shape, BF), pltpu.VMEM((depth, edges), F32), edge, edge, slope,
            pltpu.SemaphoreType.DMA((5,)), rel_sem,
        ],
        60, edge_flops + rel_flops, 12 << 20,
    )(head, tail, rel, head_rows, tail_rows, relation_ids, t_state)
    got = lax.all_to_all(part, "narrow", 0, 0, tiled=True)
    rel_1 = call(
        functools.partial(relation_kernel, 1), [((depth, edges), BF)], [VMEM, ANY], [rel_scratch, rel_sem],
        60, rel_flops, 2 * depth * types,
    )(relation_ids, rel)[0]
    moved = passed_along(low, "wide", 1)
    sums, moved, rel_1, tail, t_state = spread(got, moved, rel_1, tail, t_state)
    part, grad = call(
        second_kernel, [part_out, (tail.shape, BF)], [VMEM] * 7,
        [pltpu.VMEM(head.shape, BF), hot, edge, edge, slope],
        24, edge_flops, 9 << 20,
    )(head, h_state, sums, moved, rel_1, head_rows, tail_rows)
    got = lax.all_to_all(part, "narrow", 0, 0, tiled=True)
    grad = passed_along(grad, "wide", -1)
    head_step = call(
        head_kernel, [(head.shape, F32), ((1, hrows), F32)], [VMEM] * 3, (), 24, 0, 4 << 20
    )
    head, h_state = head_step(head, h_state, sums)
    tail, t_state = call(
        tail_end_kernel, [(tail.shape, F32), ((1, trows), F32)], [VMEM] * 3, (), 24, 0, 2 << 20
    )(tail, t_state, grad)
    sums, tail, t_state, head, h_state = spread(got, tail, t_state, head, h_state)
    head, h_state = head_step(head, h_state, sums)
    return head.T, h_state[0], tail.T, t_state[0]


def solution(mesh):
    return jax.shard_map(
        local,
        mesh=mesh,
        in_specs=(
            P("wide", None),
            P("wide"),
            P(("wide", "narrow"), None),
            P(("wide", "narrow")),
            P(),
            P(None, ("wide", "narrow")),
            P(None, ("wide", "narrow")),
            P(None, ("wide", "narrow")),
        ),
        out_specs=(P("wide", None), P("wide"), P(("wide", "narrow"), None), P(("wide", "narrow"))),
        check_vma=False,
    )
```

time: 111 us -> 97.7 us (0.88)
  the two profiles are of different devices: /device:TPU:1 before, /device:TPU:225 now
where the time goes in v2:
time: 97.7 us; the launch traced here: 97.3 us
  Pallas kernels  35.8 us (37%)
  blocking collectives  31.7 us (32%)
  waiting for transfers between devices  14.1 us (14%)
  starting transfers between devices  12 us (12%)
  local copies, waits for them, and re-layouts  2.91 us (3%)
    all_to_all x2, blocking collectives, spread(): return (lax.all_to_all(same, 'narrow', 0, 0, tiled=True), *before)  31.7 us
    pallas_call x1, Pallas kernels, local(): call(first_kernel, [part_out, (tail.shape, F32), ((1, trows), F32), (tail...  16.8 us
    ppermute x2, waiting for transfers between devices, passed_along(): lax.ppermute(value, axis, [(source, (source + steps) % count) for source...  12.5 us
    pallas_call x1, Pallas kernels, local(): call(functools.partial(relation_kernel, 1), [((depth, edges), BF)], [VMEM...  9.77 us
    all_to_all x2, starting transfers between devices, local(): got = lax.all_to_all(part, 'narrow', 0, 0, tiled=True)  8.73 us
    pallas_call x1, Pallas kernels, local(): call(second_kernel, [part_out, (tail.shape, BF)], [VMEM] * 7, [pltpu.VMEM...  5.81 us
    ppermute x2, starting transfers between devices, passed_along(): lax.ppermute(value, axis, [(source, (source + steps) % count) for source...  3.32 us
    unnamed x24, local copies, waits for them, and re-layouts  2.91 us
  transfers between devices with their start and end apart: 4, of which 2 were waited for; matrix products, arithmetic and copies ran while one was open for 0% of the time, Pallas kernels for 12%

profile of v2, /device:TPU:225, one launch (start us, length us, event | category | flops | bytes accessed | tf_op | source)
XLA Modules:
  0.0 97.3 jit_solution(15769401985314208116)
XLA Ops:
  0.6 16.8 %shard_map.111 = (bf16[8,400,128]{2,1,0:T(8,128)(2,1)}, f32[400,512]{1,0:T(8,128)}, f32[1,512]{1,0:T(1,128)}, bf16[400,512]{1,0:T(8,128)(2,1)}) custom-call(f32[400,1024]{1,0:T(8,128)} %bitcast.9, f32[400,512]{1,0:T(8,128)} %bitcast.17, bf16[400,7424]{1,0:T(8,128)(2,1)} %bitcast.14, s32[2,1024]{1,0:T(2,128)} %rows_ref.1, s32[2,1024]{1,0:T(2,128)} %tails_ref.1, ...), custom_call_target="tpu_custom_call" | custom-call | flops 9017753600 | bytes 12582912 | tf_op jit(solution)/shard_map/pallas_call | solution.py:198
  17.5 0.0 copy-start.11
  17.5 5.2 %all-to-all-start = ((bf16[8,400,128]{2,1,0:T(8,128)(2,1)}), bf16[8,400,128]{2,1,0:T(8,128)(2,1)S(1)}, u32[]{:S(2)}, u32[]{:S(2)}) async-start(bf16[8,400,128]{2,1,0:T(8,128)(2,1)} %get-tuple-element.26), calls=%async_computation | async-start | bytes 1638400 | tf_op jit(solution)/shard_map/all_to_all | solution.py:207
  22.7 0.0 copy-done.11
  22.7 0.5 collective-permute-start
  23.2 9.8 %shard_map.113.rel_ref = bf16[400,1024]{1,0:T(8,128)(2,1)} custom-call(s32[2,1024]{1,0:T(2,128)} %ids_ref.1, bf16[400,7424]{1,0:T(8,128)(2,1)} %bitcast.15), custom_call_target="tpu_custom_call" | custom-call | flops 6081740800 | bytes 5939200 | tf_op jit(solution)/shard_map/pallas_call | solution.py:208
  33.0 0.0 copy-start
  33.0 0.0 copy-start.5
  33.0 0.0 copy-start.8
  33.0 0.0 copy-start.9
  33.0 1.7 %all-to-all-done.got_ref = bf16[8,400,128]{2,1,0:T(8,128)(2,1)S(1)} async-done(((bf16[8,400,128]{2,1,0:T(8,128)(2,1)}), bf16[8,400,128]{2,1,0:T(8,128)(2,1)S(1)}, u32[]{:S(2)}, u32[]{:S(2)}) %all-to-all-start) | async-done | bytes 819232 | tf_op jit(solution)/shard_map/all_to_all | solution.py:207
  34.7 0.1 shard_map.112
  34.8 0.0 collective-permute-done.low_ref
  34.8 15.1 %all_to_all.20.sums_ref = bf16[8,400,128]{2,1,0:T(8,128)(2,1)S(1)} all-to-all(bf16[8,400,128]{2,1,0:T(8,128)(2,1)S(1)} %shard_map.112), channel_id=1, replica_groups=mesh['wide'=32,'narrow'=8] {'narrow'}, dimensions={0} | all-to-all | bytes 1638400 | tf_op jit(solution)/shard_map/all_to_all | solution.py:176
  49.9 0.0 copy-done
  49.9 0.0 copy-done.5
  50.0 5.8 %shard_map.114 = (bf16[8,400,128]{2,1,0:T(8,128)(2,1)S(1)}, bf16[400,512]{1,0:T(8,128)(2,1)S(1)}) custom-call(f32[400,1024]{1,0:T(8,128)S(1)} %bitcast.10, f32[1,1024]{1,0:T(1,128)S(1)} %bitcast.12, bf16[8,400,128]{2,1,0:T(8,128)(2,1)S(1)} %all_to_all.20.sums_ref, bf16[400,512]{1,0:T(8,128)(2,1)S(1)} %collective-permute-done.low_ref, ...), custom_call_target="tpu_custom_call" | custom-call | flops 2936012800 | bytes 9437184 | tf_op jit(solution)/shard_map/pallas_call | solution.py:214
  55.8 0.0 copy-start.4
  55.8 0.9 copy-done.4
  56.7 0.7 copy-done.7
  57.5 3.5 %all-to-all-start.2 = ((bf16[8,400,128]{2,1,0:T(8,128)(2,1)}), bf16[8,400,128]{2,1,0:T(8,128)(2,1)S(1)}, u32[]{:S(2)}, u32[]{:S(2)}) async-start(bf16[8,400,128]{2,1,0:T(8,128)(2,1)} %copy-done.4), calls=%async_computation.2 | async-start | bytes 1638400 | tf_op jit(solution)/shard_map/all_to_all | solution.py:219
  61.1 0.0 copy-start.6
  61.1 2.8 %collective-permute-start.1 = (bf16[400,512]{1,0:T(8,128)(2,1)}, bf16[400,512]{1,0:T(8,128)(2,1)S(1)}, u32[]{:S(2)}, u32[]{:S(2)}) collective-permute-start(bf16[400,512]{1,0:T(8,128)(2,1)} %copy-done.7), channel_id=1, source_target_pairs={{0,248},{8,0},{16,8},{24,16},{32,24},{40,32},{48,40},{56,48},{64,5... | collective-permute-start | bytes 1228808 | tf_op jit(solution)/shard_map/ppermute | solution.py:170
  63.9 0.4 shard_map.117
  64.3 0.0 copy-start.1
  64.3 1.2 %copy-done.1 = f32[400,1024]{1,0:T(8,128)} copy-done((f32[400,1024]{1,0:T(8,128)}, f32[400,1024]{1,0:T(8,128)S(1)}, u32[]{:S(2)}) %copy-start.1) | copy-done | bytes 1638424
  65.5 12.5 %collective-permute-done.1.grad_ref = bf16[400,512]{1,0:T(8,128)(2,1)S(1)} collective-permute-done((bf16[400,512]{1,0:T(8,128)(2,1)}, bf16[400,512]{1,0:T(8,128)(2,1)S(1)}, u32[]{:S(2)}, u32[]{:S(2)}) %collective-permute-start.1) | collective-permute-done | bytes 409632 | tf_op jit(solution)/shard_map/ppermute | solution.py:170
  78.0 1.1 %shard_map.116 = (f32[400,512]{1,0:T(8,128)}, f32[1,512]{1,0:T(1,128)}) custom-call(f32[400,512]{1,0:T(8,128)S(1)} %copy-done.3, f32[1,512]{1,0:T(1,128)S(1)} %copy-done.6, bf16[400,512]{1,0:T(8,128)(2,1)S(1)} %collective-permute-done.1.grad_ref), custom_call_target="tpu_custom_call" | custom-call | bytes 2097152 | tf_op jit(solution)/shard_map/pallas_call | solution.py:225
  79.0 0.0 all-to-all-done.2.got_ref
  79.1 0.1 shard_map.115
  79.2 16.5 %all_to_all.21.sums_ref = bf16[8,400,128]{2,1,0:T(8,128)(2,1)S(1)} all-to-all(bf16[8,400,128]{2,1,0:T(8,128)(2,1)S(1)} %shard_map.115), channel_id=1, replica_groups=mesh['wide'=32,'narrow'=8] {'narrow'}, dimensions={0} | all-to-all | bytes 1638400 | tf_op jit(solution)/shard_map/all_to_all | solution.py:176
  95.7 1.6 %shard_map.118 = (f32[400,1024]{1,0:T(8,128)}, f32[1,1024]{1,0:T(1,128)}) custom-call(f32[400,1024]{1,0:T(8,128)S(1)} %copy-done.2, f32[1,1024]{1,0:T(1,128)S(1)} %get-tuple-element.42.state_ref, bf16[8,400,128]{2,1,0:T(8,128)(2,1)S(1)} %all_to_all.21.sums_ref), custom_call_target="tpu_custom_call" | custom-call | bytes 4194304 | tf_op jit(solution)/shard_map/pallas_call | solution.py:229
  (10 shorter events, 0.0 us)
Async XLA Ops:
  17.5 5.2 %copy-start.11 = (bf16[400,512]{1,0:T(8,128)(2,1)S(1)}, bf16[400,512]{1,0:T(8,128)(2,1)}, u32[]{:S(2)}) copy-start(bf16[400,512]{1,0:T(8,128)(2,1)} %get-tuple-element.27) | copy-start | bytes 1228804
  17.5 17.2 %all-to-all-start = ((bf16[8,400,128]{2,1,0:T(8,128)(2,1)}), bf16[8,400,128]{2,1,0:T(8,128)(2,1)S(1)}, u32[]{:S(2)}, u32[]{:S(2)}) async-start(bf16[8,400,128]{2,1,0:T(8,128)(2,1)} %get-tuple-element.26), calls=%async_computation | async-start | bytes 1638400 | tf_op jit(solution)/shard_map/all_to_all | solution.py:207
  22.7 12.1 %collective-permute-start = (bf16[400,512]{1,0:T(8,128)(2,1)S(1)}, bf16[400,512]{1,0:T(8,128)(2,1)S(1)}, u32[]{:S(2)}, u32[]{:S(2)}) collective-permute-start(bf16[400,512]{1,0:T(8,128)(2,1)S(1)} %copy-done.11), channel_id=1, source_target_pairs={{0,8},{8,16},{16,24},{24,32},{32,40},{40,48},{48,56},{56,64},{64,7... | collective-permute-start | bytes 1228808 | tf_op jit(solution)/shard_map/ppermute | solution.py:170
  33.0 17.0 %copy-start = (f32[1024,400]{0,1:T(8,128)S(1)}, f32[1024,400]{0,1:T(8,128)}, u32[]{:S(2)}) copy-start(f32[1024,400]{0,1:T(8,128)} %param.8) | copy-start | bytes 4915204
  33.0 16.9 %copy-start.5 = (f32[1024]{0:T(1024)S(1)}, f32[1024]{0:T(1024)}, u32[]{:S(2)}) copy-start(f32[1024]{0:T(1024)} %param.9) | copy-start | bytes 12292
  33.0 16.9 %copy-start.8 = (s32[2,1024]{1,0:T(2,128)S(1)}, s32[2,1024]{1,0:T(2,128)}, u32[]{:S(2)}) copy-start(s32[2,1024]{1,0:T(2,128)} %rows_ref.1) | copy-start | bytes 24580
  33.0 16.9 %copy-start.9 = (s32[2,1024]{1,0:T(2,128)S(1)}, s32[2,1024]{1,0:T(2,128)}, u32[]{:S(2)}) copy-start(s32[2,1024]{1,0:T(2,128)} %tails_ref.1) | copy-start | bytes 24580
  34.7 15.3 %copy-start.10 = (bf16[400,1024]{1,0:T(8,128)(2,1)S(1)}, bf16[400,1024]{1,0:T(8,128)(2,1)}, u32[]{:S(2)}) copy-start(bf16[400,1024]{1,0:T(8,128)(2,1)} %shard_map.113.rel_ref) | copy-start | bytes 2457604
  55.8 1.0 copy-start.4
  56.7 0.8 copy-start.7
  57.5 21.6 %all-to-all-start.2 = ((bf16[8,400,128]{2,1,0:T(8,128)(2,1)}), bf16[8,400,128]{2,1,0:T(8,128)(2,1)S(1)}, u32[]{:S(2)}, u32[]{:S(2)}) async-start(bf16[8,400,128]{2,1,0:T(8,128)(2,1)} %copy-done.4), calls=%async_computation.2 | async-start | bytes 1638400 | tf_op jit(solution)/shard_map/all_to_all | solution.py:219
  61.0 16.9 %copy-start.3 = (f32[400,512]{1,0:T(8,128)S(1)}, f32[400,512]{1,0:T(8,128)}, u32[]{:S(2)}) copy-start(f32[400,512]{1,0:T(8,128)} %get-tuple-element.34.tail_ref) | copy-start | bytes 2457604
  61.1 16.9 %copy-start.6 = (f32[1,512]{1,0:T(1,128)S(1)}, f32[1,512]{1,0:T(1,128)}, u32[]{:S(2)}) copy-start(f32[1,512]{1,0:T(1,128)} %get-tuple-element.35.state_ref) | copy-start | bytes 6148
  61.1 16.9 %collective-permute-start.1 = (bf16[400,512]{1,0:T(8,128)(2,1)}, bf16[400,512]{1,0:T(8,128)(2,1)S(1)}, u32[]{:S(2)}, u32[]{:S(2)}) collective-permute-start(bf16[400,512]{1,0:T(8,128)(2,1)} %copy-done.7), channel_id=1, source_target_pairs={{0,248},{8,0},{16,8},{24,16},{32,24},{40,32},{48,40},{56,48},{64,5... | collective-permute-start | bytes 1228808 | tf_op jit(solution)/shard_map/ppermute | solution.py:170
  64.3 1.2 %copy-start.1 = (f32[400,1024]{1,0:T(8,128)}, f32[400,1024]{1,0:T(8,128)S(1)}, u32[]{:S(2)}) copy-start(f32[400,1024]{1,0:T(8,128)S(1)} %get-tuple-element.41.head_ref) | copy-start | bytes 4915204
  79.0 16.7 %copy-start.2 = (f32[400,1024]{1,0:T(8,128)S(1)}, f32[400,1024]{1,0:T(8,128)}, u32[]{:S(2)}) copy-start(f32[400,1024]{1,0:T(8,128)} %copy-done.1) | copy-start | bytes 4915204

commit v3 on v2

--- a/solution.py
+++ b/solution.py
@@ -13,8 +13,10 @@
 VMEM = pl.BlockSpec(memory_space=pltpu.VMEM)
 ANY = pl.BlockSpec(memory_space=pl.ANY)
 LANES = 128
-TILE = 512
-PIECES = 8
+TILE = 1024
+CUTS = (4, 12, 30)
+PIECES = len(CUTS) + 1
+SPAN = 512
 
 
 def call(kernel, outs, ins, scratch=(), mib=32, flops=0, nbytes=0, out_specs=None):
@@ -39,9 +41,8 @@
 
 
 def pieces_of(width):
-    blocks = width // LANES
-    each = -(-blocks // PIECES)
-    return [(p * each * LANES, min(each, blocks - p * each) * LANES) for p in range(PIECES)]
+    ends = [0, *(c * LANES for c in CUTS), width]
+    return [(a, b - a) for a, b in zip(ends, ends[1:])]
 
 
 def relation_copies(rel_hbm, rel_ref, sem):
@@ -86,8 +87,10 @@
 
 def scatter(part_ref, edge_ref, hot_ref):
     width = part_ref.shape[2]
-    for n in range(part_ref.shape[0]):
-        part_ref[n] = dot(edge_ref[...], hot_ref[n * width : (n + 1) * width, :], ((1,), (1,))).astype(BF)
+    for first in range(0, hot_ref.shape[0], SPAN):
+        part = dot(edge_ref[...], hot_ref[first : first + SPAN, :], ((1,), (1,))).astype(BF)
+        for n in range(SPAN // width):
+            part_ref[first // width + n] = part[:, n * width : (n + 1) * width]
 
 
 def stepped(table, state, grad):
@@ -99,25 +102,19 @@
     head_hbm, tail_hbm, rel_hbm, rows_hbm, tails_hbm, ids_hbm, state_ref, part_ref, tail_out, state_out, low_out,
     head_ref, tail_ref, rel_ref, rows_ref, tails_ref, ids_ref, hot_ref, low_ref, h_ref, edge_ref, q_ref, sl_ref, sem, rel_sem,
 ):
-    pairs = [(rows_hbm, rows_ref), (ids_hbm, ids_ref), (head_hbm, head_ref), (tails_hbm, tails_ref), (tail_hbm, tail_ref)]
+    pairs = [(ids_hbm, ids_ref), (rows_hbm, rows_ref), (head_hbm, head_ref), (tails_hbm, tails_ref), (tail_hbm, tail_ref)]
     copies = [pltpu.make_async_copy(a, b, sem.at[i]) for i, (a, b) in enumerate(pairs)]
     rel_copies = relation_copies(rel_hbm, rel_ref, rel_sem)
-    for copy in copies + rel_copies:
+    for copy in copies[:1] + rel_copies + copies[1:]:
         copy.start()
     copies[0].wait()
+    r = relation_tile(rel_ref, ids_ref[0:1, :], rel_copies)
+    for copy in copies[1:]:
+        copy.wait()
     hot_ref[...] = one_hot(rows_ref[0:1, :], 0, head_ref.shape[1])
-    copies[1].wait()
-    copies[2].wait()
-    h_ref[...] = dot(head_ref[...].astype(BF), hot_ref[...])
-    copies[3].wait()
-    copies[4].wait()
+    h = dot(head_ref[...].astype(BF), hot_ref[...])
     low_ref[...] = tail_ref[...].astype(BF)
-    for t in range(ids_ref.shape[1] // TILE):
-        cols = pl.ds(t * TILE, TILE)
-        r = relation_tile(rel_ref, ids_ref[0:1, cols], None if t else rel_copies)
-        q_ref[:, cols], sl_ref[:, cols], edge_ref[:, cols] = edge_tile(
-            h_ref[:, cols], r, low_ref[...], tails_ref[0:1, cols]
-        )
+    q_ref[...], sl_ref[...], edge_ref[...] = edge_tile(h, r, low_ref[...], tails_ref[0:1, :])
     scatter(part_ref, edge_ref, hot_ref)
     tail, state_out[...] = stepped(tail_ref[...], state_ref[...], dot(q_ref[...], sl_ref[...], ((1,), (1,))))
     tail_out[...] = tail

time: 97.7 us -> 92.9 us (0.951)
  Pallas kernels: 35.8 us -> 30.5 us
    pallas_call x1, Pallas kernels: 16.8 us -> 13.5 us  [local(): call(first_kernel, [part_out, (tail.shape, F32), ((1, trows), F32), (tail...]
    pallas_call x1, Pallas kernels: 5.81 us -> 4.27 us  [local(): call(second_kernel, [part_out, (tail.shape, BF)], [VMEM] * 7, [pltpu.VMEM...]
where the time goes in v3:
time: 92.9 us; the launch traced here: 92.5 us
  blocking collectives  31.7 us (34%)
  Pallas kernels  30.5 us (33%)
  waiting for transfers between devices  14.6 us (16%)
  starting transfers between devices  12 us (13%)
  local copies, waits for them, and re-layouts  2.91 us (3%)
    all_to_all x2, blocking collectives, spread(): return (lax.all_to_all(same, 'narrow', 0, 0, tiled=True), *before)  31.7 us
    pallas_call x1, Pallas kernels, local(): call(first_kernel, [part_out, (tail.shape, F32), ((1, trows), F32), (tail...  13.5 us
    ppermute x2, waiting for transfers between devices, passed_along(): lax.ppermute(value, axis, [(source, (source + steps) % count) for source...  12.5 us
    pallas_call x1, Pallas kernels, local(): call(functools.partial(relation_kernel, 1), [((depth, edges), BF)], [VMEM...  9.34 us
    all_to_all x2, starting transfers between devices, local(): got = lax.all_to_all(part, 'narrow', 0, 0, tiled=True)  8.74 us
    pallas_call x1, Pallas kernels, local(): call(second_kernel, [part_out, (tail.shape, BF)], [VMEM] * 7, [pltpu.VMEM...  4.27 us
    ppermute x2, starting transfers between devices, passed_along(): lax.ppermute(value, axis, [(source, (source + steps) % count) for source...  3.31 us
    unnamed x24, local copies, waits for them, and re-layouts  2.91 us
  transfers between devices with their start and end apart: 4, of which 2 were waited for; matrix products, arithmetic and copies ran while one was open for 0% of the time, Pallas kernels for 12%

profile of v3, /device:TPU:225, one launch (start us, length us, event | category | flops | bytes accessed | tf_op | source)
XLA Modules:
  0.0 92.5 jit_solution(1954415139588417536)
XLA Ops:
  0.6 13.5 %shard_map.111 = (bf16[8,400,128]{2,1,0:T(8,128)(2,1)}, f32[400,512]{1,0:T(8,128)}, f32[1,512]{1,0:T(1,128)}, bf16[400,512]{1,0:T(8,128)(2,1)}) custom-call(f32[400,1024]{1,0:T(8,128)} %bitcast.9, f32[400,512]{1,0:T(8,128)} %bitcast.17, bf16[400,7424]{1,0:T(8,128)(2,1)} %bitcast.14, s32[2,1024]{1,0:T(2,128)} %rows_ref.1, s32[2,1024]{1,0:T(2,128)} %tails_ref.1, ...), custom_call_target="tpu_custom_call" | custom-call | flops 9017753600 | bytes 12582912 | tf_op jit(solution)/shard_map/pallas_call | solution.py:195
  14.2 0.0 copy-start.11
  14.2 5.2 %all-to-all-start = ((bf16[8,400,128]{2,1,0:T(8,128)(2,1)}), bf16[8,400,128]{2,1,0:T(8,128)(2,1)S(1)}, u32[]{:S(2)}, u32[]{:S(2)}) async-start(bf16[8,400,128]{2,1,0:T(8,128)(2,1)} %get-tuple-element.26), calls=%async_computation | async-start | bytes 1638400 | tf_op jit(solution)/shard_map/all_to_all | solution.py:204
  19.4 0.0 copy-done.11
  19.4 0.5 collective-permute-start
  19.9 9.3 %shard_map.113.rel_ref = bf16[400,1024]{1,0:T(8,128)(2,1)} custom-call(s32[2,1024]{1,0:T(2,128)} %ids_ref.1, bf16[400,7424]{1,0:T(8,128)(2,1)} %bitcast.15), custom_call_target="tpu_custom_call" | custom-call | flops 6081740800 | bytes 5939200 | tf_op jit(solution)/shard_map/pallas_call | solution.py:205
  29.3 0.0 copy-start
  29.3 0.0 copy-start.5
  29.3 0.0 copy-start.8
  29.3 0.0 copy-start.9
  29.3 2.1 %all-to-all-done.got_ref = bf16[8,400,128]{2,1,0:T(8,128)(2,1)S(1)} async-done(((bf16[8,400,128]{2,1,0:T(8,128)(2,1)}), bf16[8,400,128]{2,1,0:T(8,128)(2,1)S(1)}, u32[]{:S(2)}, u32[]{:S(2)}) %all-to-all-start) | async-done | bytes 819232 | tf_op jit(solution)/shard_map/all_to_all | solution.py:204
  31.4 0.1 shard_map.112
  31.5 0.0 collective-permute-done.low_ref
  31.5 15.1 %all_to_all.20.sums_ref = bf16[8,400,128]{2,1,0:T(8,128)(2,1)S(1)} all-to-all(bf16[8,400,128]{2,1,0:T(8,128)(2,1)S(1)} %shard_map.112), channel_id=1, replica_groups=mesh['wide'=32,'narrow'=8] {'narrow'}, dimensions={0} | all-to-all | bytes 1638400 | tf_op jit(solution)/shard_map/all_to_all | solution.py:173
  46.6 0.0 copy-done
  46.7 4.3 %shard_map.114 = (bf16[8,400,128]{2,1,0:T(8,128)(2,1)S(1)}, bf16[400,512]{1,0:T(8,128)(2,1)S(1)}) custom-call(f32[400,1024]{1,0:T(8,128)S(1)} %bitcast.10, f32[1,1024]{1,0:T(1,128)S(1)} %bitcast.12, bf16[8,400,128]{2,1,0:T(8,128)(2,1)S(1)} %all_to_all.20.sums_ref, bf16[400,512]{1,0:T(8,128)(2,1)S(1)} %collective-permute-done.low_ref, ...), custom_call_target="tpu_custom_call" | custom-call | flops 2936012800 | bytes 9437184 | tf_op jit(solution)/shard_map/pallas_call | solution.py:211
  50.9 0.0 copy-start.4
  51.0 0.9 %copy-done.4 = bf16[8,400,128]{2,1,0:T(8,128)(2,1)} copy-done((bf16[8,400,128]{2,1,0:T(8,128)(2,1)}, bf16[8,400,128]{2,1,0:T(8,128)(2,1)S(1)}, u32[]{:S(2)}) %copy-start.4) | copy-done | bytes 819224
  51.9 0.7 copy-done.7
  52.7 3.5 %all-to-all-start.2 = ((bf16[8,400,128]{2,1,0:T(8,128)(2,1)}), bf16[8,400,128]{2,1,0:T(8,128)(2,1)S(1)}, u32[]{:S(2)}, u32[]{:S(2)}) async-start(bf16[8,400,128]{2,1,0:T(8,128)(2,1)} %copy-done.4), calls=%async_computation.2 | async-start | bytes 1638400 | tf_op jit(solution)/shard_map/all_to_all | solution.py:216
  56.2 0.0 copy-start.6
  56.2 2.8 %collective-permute-start.1 = (bf16[400,512]{1,0:T(8,128)(2,1)}, bf16[400,512]{1,0:T(8,128)(2,1)S(1)}, u32[]{:S(2)}, u32[]{:S(2)}) collective-permute-start(bf16[400,512]{1,0:T(8,128)(2,1)} %copy-done.7), channel_id=1, source_target_pairs={{0,248},{8,0},{16,8},{24,16},{32,24},{40,32},{48,40},{56,48},{64,5... | collective-permute-start | bytes 1228808 | tf_op jit(solution)/shard_map/ppermute | solution.py:167
  59.0 0.4 shard_map.117
  59.5 0.0 copy-start.1
  59.5 1.2 %copy-done.1 = f32[400,1024]{1,0:T(8,128)} copy-done((f32[400,1024]{1,0:T(8,128)}, f32[400,1024]{1,0:T(8,128)S(1)}, u32[]{:S(2)}) %copy-start.1) | copy-done | bytes 1638424
  60.6 12.5 %collective-permute-done.1.grad_ref = bf16[400,512]{1,0:T(8,128)(2,1)S(1)} collective-permute-done((bf16[400,512]{1,0:T(8,128)(2,1)}, bf16[400,512]{1,0:T(8,128)(2,1)S(1)}, u32[]{:S(2)}, u32[]{:S(2)}) %collective-permute-start.1) | collective-permute-done | bytes 409632 | tf_op jit(solution)/shard_map/ppermute | solution.py:167
  73.1 0.0 copy-done.3
  73.1 1.1 %shard_map.116 = (f32[400,512]{1,0:T(8,128)}, f32[1,512]{1,0:T(1,128)}) custom-call(f32[400,512]{1,0:T(8,128)S(1)} %copy-done.3, f32[1,512]{1,0:T(1,128)S(1)} %copy-done.6, bf16[400,512]{1,0:T(8,128)(2,1)S(1)} %collective-permute-done.1.grad_ref), custom_call_target="tpu_custom_call" | custom-call | bytes 2097152 | tf_op jit(solution)/shard_map/pallas_call | solution.py:222
  74.2 0.0 all-to-all-done.2.got_ref
  74.2 0.1 shard_map.115
  74.3 16.5 %all_to_all.21.sums_ref = bf16[8,400,128]{2,1,0:T(8,128)(2,1)S(1)} all-to-all(bf16[8,400,128]{2,1,0:T(8,128)(2,1)S(1)} %shard_map.115), channel_id=1, replica_groups=mesh['wide'=32,'narrow'=8] {'narrow'}, dimensions={0} | all-to-all | bytes 1638400 | tf_op jit(solution)/shard_map/all_to_all | solution.py:173
  90.9 1.6 %shard_map.118 = (f32[400,1024]{1,0:T(8,128)}, f32[1,1024]{1,0:T(1,128)}) custom-call(f32[400,1024]{1,0:T(8,128)S(1)} %copy-done.2, f32[1,1024]{1,0:T(1,128)S(1)} %get-tuple-element.42.state_ref, bf16[8,400,128]{2,1,0:T(8,128)(2,1)S(1)} %all_to_all.21.sums_ref), custom_call_target="tpu_custom_call" | custom-call | bytes 4194304 | tf_op jit(solution)/shard_map/pallas_call | solution.py:226
  (10 shorter events, 0.0 us)
Async XLA Ops:
  14.2 5.2 %copy-start.11 = (bf16[400,512]{1,0:T(8,128)(2,1)S(1)}, bf16[400,512]{1,0:T(8,128)(2,1)}, u32[]{:S(2)}) copy-start(bf16[400,512]{1,0:T(8,128)(2,1)} %get-tuple-element.27) | copy-start | bytes 1228804
  14.2 17.2 %all-to-all-start = ((bf16[8,400,128]{2,1,0:T(8,128)(2,1)}), bf16[8,400,128]{2,1,0:T(8,128)(2,1)S(1)}, u32[]{:S(2)}, u32[]{:S(2)}) async-start(bf16[8,400,128]{2,1,0:T(8,128)(2,1)} %get-tuple-element.26), calls=%async_computation | async-start | bytes 1638400 | tf_op jit(solution)/shard_map/all_to_all | solution.py:204
  19.4 12.1 %collective-permute-start = (bf16[400,512]{1,0:T(8,128)(2,1)S(1)}, bf16[400,512]{1,0:T(8,128)(2,1)S(1)}, u32[]{:S(2)}, u32[]{:S(2)}) collective-permute-start(bf16[400,512]{1,0:T(8,128)(2,1)S(1)} %copy-done.11), channel_id=1, source_target_pairs={{0,8},{8,16},{16,24},{24,32},{32,40},{40,48},{48,56},{56,64},{64,7... | collective-permute-start | bytes 1228808 | tf_op jit(solution)/shard_map/ppermute | solution.py:167
  29.3 17.4 %copy-start = (f32[1024,400]{0,1:T(8,128)S(1)}, f32[1024,400]{0,1:T(8,128)}, u32[]{:S(2)}) copy-start(f32[1024,400]{0,1:T(8,128)} %param.8) | copy-start | bytes 4915204
  29.3 17.4 %copy-start.5 = (f32[1024]{0:T(1024)S(1)}, f32[1024]{0:T(1024)}, u32[]{:S(2)}) copy-start(f32[1024]{0:T(1024)} %param.9) | copy-start | bytes 12292
  29.3 17.4 %copy-start.8 = (s32[2,1024]{1,0:T(2,128)S(1)}, s32[2,1024]{1,0:T(2,128)}, u32[]{:S(2)}) copy-start(s32[2,1024]{1,0:T(2,128)} %rows_ref.1) | copy-start | bytes 24580
  29.3 17.4 %copy-start.9 = (s32[2,1024]{1,0:T(2,128)S(1)}, s32[2,1024]{1,0:T(2,128)}, u32[]{:S(2)}) copy-start(s32[2,1024]{1,0:T(2,128)} %tails_ref.1) | copy-start | bytes 24580
  31.4 15.3 %copy-start.10 = (bf16[400,1024]{1,0:T(8,128)(2,1)S(1)}, bf16[400,1024]{1,0:T(8,128)(2,1)}, u32[]{:S(2)}) copy-start(bf16[400,1024]{1,0:T(8,128)(2,1)} %shard_map.113.rel_ref) | copy-start | bytes 2457604
  50.9 1.0 %copy-start.4 = (bf16[8,400,128]{2,1,0:T(8,128)(2,1)}, bf16[8,400,128]{2,1,0:T(8,128)(2,1)S(1)}, u32[]{:S(2)}) copy-start(bf16[8,400,128]{2,1,0:T(8,128)(2,1)S(1)} %get-tuple-element.33) | copy-start | bytes 2457604
  51.9 0.8 copy-start.7
  52.7 21.6 %all-to-all-start.2 = ((bf16[8,400,128]{2,1,0:T(8,128)(2,1)}), bf16[8,400,128]{2,1,0:T(8,128)(2,1)S(1)}, u32[]{:S(2)}, u32[]{:S(2)}) async-start(bf16[8,400,128]{2,1,0:T(8,128)(2,1)} %copy-done.4), calls=%async_computation.2 | async-start | bytes 1638400 | tf_op jit(solution)/shard_map/all_to_all | solution.py:216
  56.2 16.9 %copy-start.3 = (f32[400,512]{1,0:T(8,128)S(1)}, f32[400,512]{1,0:T(8,128)}, u32[]{:S(2)}) copy-start(f32[400,512]{1,0:T(8,128)} %get-tuple-element.34.tail_ref) | copy-start | bytes 2457604
  56.2 16.9 %copy-start.6 = (f32[1,512]{1,0:T(1,128)S(1)}, f32[1,512]{1,0:T(1,128)}, u32[]{:S(2)}) copy-start(f32[1,512]{1,0:T(1,128)} %get-tuple-element.35.state_ref) | copy-start | bytes 6148
  56.2 16.9 %collective-permute-start.1 = (bf16[400,512]{1,0:T(8,128)(2,1)}, bf16[400,512]{1,0:T(8,128)(2,1)S(1)}, u32[]{:S(2)}, u32[]{:S(2)}) collective-permute-start(bf16[400,512]{1,0:T(8,128)(2,1)} %copy-done.7), channel_id=1, source_target_pairs={{0,248},{8,0},{16,8},{24,16},{32,24},{40,32},{48,40},{56,48},{64,5... | collective-permute-start | bytes 1228808 | tf_op jit(solution)/shard_map/ppermute | solution.py:167
  59.5 1.2 %copy-start.1 = (f32[400,1024]{1,0:T(8,128)}, f32[400,1024]{1,0:T(8,128)S(1)}, u32[]{:S(2)}) copy-start(f32[400,1024]{1,0:T(8,128)S(1)} %get-tuple-element.41.head_ref) | copy-start | bytes 4915204
  74.2 16.7 %copy-start.2 = (f32[400,1024]{1,0:T(8,128)S(1)}, f32[400,1024]{1,0:T(8,128)}, u32[]{:S(2)}) copy-start(f32[400,1024]{1,0:T(8,128)} %copy-done.1) | copy-start | bytes 4915204

commit v4 on v3

--- a/solution.py
+++ b/solution.py
@@ -115,10 +115,18 @@
     h = dot(head_ref[...].astype(BF), hot_ref[...])
     low_ref[...] = tail_ref[...].astype(BF)
     q_ref[...], sl_ref[...], edge_ref[...] = edge_tile(h, r, low_ref[...], tails_ref[0:1, :])
+    tail, state_out[...] = stepped(tail_ref[...], state_ref[...], dot(q_ref[...], sl_ref[...], ((1,), (1,))))
+    tail_ref[...] = tail
+    low_ref[...] = tail.astype(BF)
+    outs = [
+        pltpu.make_async_copy(low_ref, low_out, sem.at[0]),
+        pltpu.make_async_copy(tail_ref, tail_out, sem.at[1]),
+    ]
+    for copy in outs:
+        copy.start()
     scatter(part_ref, edge_ref, hot_ref)
-    tail, state_out[...] = stepped(tail_ref[...], state_ref[...], dot(q_ref[...], sl_ref[...], ((1,), (1,))))
-    tail_out[...] = tail
-    low_out[...] = tail.astype(BF)
+    for copy in outs:
+        copy.wait()
 
 
 def sum_kernel(got_ref, out_ref):
@@ -199,7 +207,7 @@
             hot, pltpu.VMEM(tail.shape, BF), pltpu.VMEM((depth, edges), F32), edge, edge, slope,
             pltpu.SemaphoreType.DMA((5,)), rel_sem,
         ],
-        60, edge_flops + rel_flops, 12 << 20,
+        60, edge_flops + rel_flops, 12 << 20, [VMEM, ANY, VMEM, ANY],
     )(head, tail, rel, head_rows, tail_rows, relation_ids, t_state)
     got = lax.all_to_all(part, "narrow", 0, 0, tiled=True)
     rel_1 = call(

time: 92.9 us -> 93 us (level)
  no operation moved by 1% of the time
where the time goes in v4:
time: 93 us; the launch traced here: 92.6 us
  blocking collectives  31.7 us (34%)
  Pallas kernels  30.6 us (33%)
  waiting for transfers between devices  14.6 us (16%)
  starting transfers between devices  12 us (13%)
  local copies, waits for them, and re-layouts  2.91 us (3%)
    all_to_all x2, blocking collectives, spread(): return (lax.all_to_all(same, 'narrow', 0, 0, tiled=True), *before)  31.7 us
    pallas_call x1, Pallas kernels, local(): call(first_kernel, [part_out, (tail.shape, F32), ((1, trows), F32), (tail...  13.6 us
    ppermute x2, waiting for transfers between devices, passed_along(): lax.ppermute(value, axis, [(source, (source + steps) % count) for source...  12.5 us
    pallas_call x1, Pallas kernels, local(): call(functools.partial(relation_kernel, 1), [((depth, edges), BF)], [VMEM...  9.34 us
    all_to_all x2, starting transfers between devices, local(): got = lax.all_to_all(part, 'narrow', 0, 0, tiled=True)  8.73 us
    pallas_call x1, Pallas kernels, local(): call(second_kernel, [part_out, (tail.shape, BF)], [VMEM] * 7, [pltpu.VMEM...  4.27 us
    ppermute x2, starting transfers between devices, passed_along(): lax.ppermute(value, axis, [(source, (source + steps) % count) for source...  3.32 us
    unnamed x24, local copies, waits for them, and re-layouts  2.91 us
  transfers between devices with their start and end apart: 4, of which 2 were waited for; matrix products, arithmetic and copies ran while one was open for 0% of the time, Pallas kernels for 12%

profile of v4, /device:TPU:225, one launch (start us, length us, event | category | flops | bytes accessed | tf_op | source)
XLA Modules:
  0.0 92.6 jit_solution(17861740466162484845)
XLA Ops:
  0.6 13.6 %shard_map.111 = (bf16[8,400,128]{2,1,0:T(8,128)(2,1)}, f32[400,512]{1,0:T(8,128)}, f32[1,512]{1,0:T(1,128)}, bf16[400,512]{1,0:T(8,128)(2,1)}) custom-call(f32[400,1024]{1,0:T(8,128)} %bitcast.9, f32[400,512]{1,0:T(8,128)} %bitcast.17, bf16[400,7424]{1,0:T(8,128)(2,1)} %bitcast.14, s32[2,1024]{1,0:T(2,128)} %rows_ref.1, s32[2,1024]{1,0:T(2,128)} %tails_ref.1, ...), custom_call_target="tpu_custom_call" | custom-call | flops 9017753600 | bytes 12582912 | tf_op jit(solution)/shard_map/pallas_call | solution.py:203
  14.3 0.0 copy-start.11
  14.3 5.2 %all-to-all-start = ((bf16[8,400,128]{2,1,0:T(8,128)(2,1)}), bf16[8,400,128]{2,1,0:T(8,128)(2,1)S(1)}, u32[]{:S(2)}, u32[]{:S(2)}) async-start(bf16[8,400,128]{2,1,0:T(8,128)(2,1)} %get-tuple-element.26), calls=%async_computation | async-start | bytes 1638400 | tf_op jit(solution)/shard_map/all_to_all | solution.py:212
  19.5 0.0 copy-done.11
  19.5 0.5 collective-permute-start
  20.0 9.3 %shard_map.113.rel_ref = bf16[400,1024]{1,0:T(8,128)(2,1)} custom-call(s32[2,1024]{1,0:T(2,128)} %ids_ref.1, bf16[400,7424]{1,0:T(8,128)(2,1)} %bitcast.15), custom_call_target="tpu_custom_call" | custom-call | flops 6081740800 | bytes 5939200 | tf_op jit(solution)/shard_map/pallas_call | solution.py:213
  29.3 0.0 copy-start
  29.4 0.0 copy-start.5
  29.4 0.0 copy-start.8
  29.4 0.0 copy-start.9
  29.4 2.1 %all-to-all-done.got_ref = bf16[8,400,128]{2,1,0:T(8,128)(2,1)S(1)} async-done(((bf16[8,400,128]{2,1,0:T(8,128)(2,1)}), bf16[8,400,128]{2,1,0:T(8,128)(2,1)S(1)}, u32[]{:S(2)}, u32[]{:S(2)}) %all-to-all-start) | async-done | bytes 819232 | tf_op jit(solution)/shard_map/all_to_all | solution.py:212
  31.5 0.1 shard_map.112
  31.6 0.0 collective-permute-done.low_ref
  31.6 15.1 %all_to_all.20.sums_ref = bf16[8,400,128]{2,1,0:T(8,128)(2,1)S(1)} all-to-all(bf16[8,400,128]{2,1,0:T(8,128)(2,1)S(1)} %shard_map.112), channel_id=1, replica_groups=mesh['wide'=32,'narrow'=8] {'narrow'}, dimensions={0} | all-to-all | bytes 1638400 | tf_op jit(solution)/shard_map/all_to_all | solution.py:181
  46.7 0.0 copy-done
  46.7 0.0 copy-done.9
  46.7 0.0 copy-done.10
  46.7 4.3 %shard_map.114 = (bf16[8,400,128]{2,1,0:T(8,128)(2,1)S(1)}, bf16[400,512]{1,0:T(8,128)(2,1)S(1)}) custom-call(f32[400,1024]{1,0:T(8,128)S(1)} %bitcast.10, f32[1,1024]{1,0:T(1,128)S(1)} %bitcast.12, bf16[8,400,128]{2,1,0:T(8,128)(2,1)S(1)} %all_to_all.20.sums_ref, bf16[400,512]{1,0:T(8,128)(2,1)S(1)} %collective-permute-done.low_ref, ...), custom_call_target="tpu_custom_call" | custom-call | flops 2936012800 | bytes 9437184 | tf_op jit(solution)/shard_map/pallas_call | solution.py:219
  51.0 0.9 %copy-done.4 = bf16[8,400,128]{2,1,0:T(8,128)(2,1)} copy-done((bf16[8,400,128]{2,1,0:T(8,128)(2,1)}, bf16[8,400,128]{2,1,0:T(8,128)(2,1)S(1)}, u32[]{:S(2)}) %copy-start.4) | copy-done | bytes 819224
  52.0 0.7 copy-done.7
  52.7 3.5 %all-to-all-start.2 = ((bf16[8,400,128]{2,1,0:T(8,128)(2,1)}), bf16[8,400,128]{2,1,0:T(8,128)(2,1)S(1)}, u32[]{:S(2)}, u32[]{:S(2)}) async-start(bf16[8,400,128]{2,1,0:T(8,128)(2,1)} %copy-done.4), calls=%async_computation.2 | async-start | bytes 1638400 | tf_op jit(solution)/shard_map/all_to_all | solution.py:224
  56.3 0.0 copy-start.6
  56.3 2.8 %collective-permute-start.1 = (bf16[400,512]{1,0:T(8,128)(2,1)}, bf16[400,512]{1,0:T(8,128)(2,1)S(1)}, u32[]{:S(2)}, u32[]{:S(2)}) collective-permute-start(bf16[400,512]{1,0:T(8,128)(2,1)} %copy-done.7), channel_id=1, source_target_pairs={{0,248},{8,0},{16,8},{24,16},{32,24},{40,32},{48,40},{56,48},{64,5... | collective-permute-start | bytes 1228808 | tf_op jit(solution)/shard_map/ppermute | solution.py:175
  59.1 0.4 shard_map.117
  59.5 0.0 copy-start.1
  59.6 1.2 %copy-done.1 = f32[400,1024]{1,0:T(8,128)} copy-done((f32[400,1024]{1,0:T(8,128)}, f32[400,1024]{1,0:T(8,128)S(1)}, u32[]{:S(2)}) %copy-start.1) | copy-done | bytes 1638424
  60.7 12.5 %collective-permute-done.1.grad_ref = bf16[400,512]{1,0:T(8,128)(2,1)S(1)} collective-permute-done((bf16[400,512]{1,0:T(8,128)(2,1)}, bf16[400,512]{1,0:T(8,128)(2,1)S(1)}, u32[]{:S(2)}, u32[]{:S(2)}) %collective-permute-start.1) | collective-permute-done | bytes 409632 | tf_op jit(solution)/shard_map/ppermute | solution.py:175
  73.2 1.1 %shard_map.116 = (f32[400,512]{1,0:T(8,128)}, f32[1,512]{1,0:T(1,128)}) custom-call(f32[400,512]{1,0:T(8,128)S(1)} %copy-done.3, f32[1,512]{1,0:T(1,128)S(1)} %copy-done.6, bf16[400,512]{1,0:T(8,128)(2,1)S(1)} %collective-permute-done.1.grad_ref), custom_call_target="tpu_custom_call" | custom-call | bytes 2097152 | tf_op jit(solution)/shard_map/pallas_call | solution.py:230
  74.3 0.0 all-to-all-done.2.got_ref
  74.3 0.1 shard_map.115
  74.4 16.5 %all_to_all.21.sums_ref = bf16[8,400,128]{2,1,0:T(8,128)(2,1)S(1)} all-to-all(bf16[8,400,128]{2,1,0:T(8,128)(2,1)S(1)} %shard_map.115), channel_id=1, replica_groups=mesh['wide'=32,'narrow'=8] {'narrow'}, dimensions={0} | all-to-all | bytes 1638400 | tf_op jit(solution)/shard_map/all_to_all | solution.py:181
  90.9 1.6 %shard_map.118 = (f32[400,1024]{1,0:T(8,128)}, f32[1,1024]{1,0:T(1,128)}) custom-call(f32[400,1024]{1,0:T(8,128)S(1)} %copy-done.2, f32[1,1024]{1,0:T(1,128)S(1)} %get-tuple-element.42.state_ref, bf16[8,400,128]{2,1,0:T(8,128)(2,1)S(1)} %all_to_all.21.sums_ref), custom_call_target="tpu_custom_call" | custom-call | bytes 4194304 | tf_op jit(solution)/shard_map/pallas_call | solution.py:234
  (10 shorter events, 0.0 us)
Async XLA Ops:
  14.3 5.2 %copy-start.11 = (bf16[400,512]{1,0:T(8,128)(2,1)S(1)}, bf16[400,512]{1,0:T(8,128)(2,1)}, u32[]{:S(2)}) copy-start(bf16[400,512]{1,0:T(8,128)(2,1)} %get-tuple-element.27) | copy-start | bytes 1228804
  14.3 17.2 %all-to-all-start = ((bf16[8,400,128]{2,1,0:T(8,128)(2,1)}), bf16[8,400,128]{2,1,0:T(8,128)(2,1)S(1)}, u32[]{:S(2)}, u32[]{:S(2)}) async-start(bf16[8,400,128]{2,1,0:T(8,128)(2,1)} %get-tuple-element.26), calls=%async_computation | async-start | bytes 1638400 | tf_op jit(solution)/shard_map/all_to_all | solution.py:212
  19.5 12.1 %collective-permute-start = (bf16[400,512]{1,0:T(8,128)(2,1)S(1)}, bf16[400,512]{1,0:T(8,128)(2,1)S(1)}, u32[]{:S(2)}, u32[]{:S(2)}) collective-permute-start(bf16[400,512]{1,0:T(8,128)(2,1)S(1)} %copy-done.11), channel_id=1, source_target_pairs={{0,8},{8,16},{16,24},{24,32},{32,40},{40,48},{48,56},{56,64},{64,7... | collective-permute-start | bytes 1228808 | tf_op jit(solution)/shard_map/ppermute | solution.py:175
  29.3 17.4 %copy-start = (f32[1024,400]{0,1:T(8,128)S(1)}, f32[1024,400]{0,1:T(8,128)}, u32[]{:S(2)}) copy-start(f32[1024,400]{0,1:T(8,128)} %param.8) | copy-start | bytes 4915204
  29.4 17.4 %copy-start.5 = (f32[1024]{0:T(1024)S(1)}, f32[1024]{0:T(1024)}, u32[]{:S(2)}) copy-start(f32[1024]{0:T(1024)} %param.9) | copy-start | bytes 12292
  29.4 17.4 %copy-start.8 = (s32[2,1024]{1,0:T(2,128)S(1)}, s32[2,1024]{1,0:T(2,128)}, u32[]{:S(2)}) copy-start(s32[2,1024]{1,0:T(2,128)} %rows_ref.1) | copy-start | bytes 24580
  29.4 17.3 %copy-start.9 = (s32[2,1024]{1,0:T(2,128)S(1)}, s32[2,1024]{1,0:T(2,128)}, u32[]{:S(2)}) copy-start(s32[2,1024]{1,0:T(2,128)} %tails_ref.1) | copy-start | bytes 24580
  31.5 15.3 %copy-start.10 = (bf16[400,1024]{1,0:T(8,128)(2,1)S(1)}, bf16[400,1024]{1,0:T(8,128)(2,1)}, u32[]{:S(2)}) copy-start(bf16[400,1024]{1,0:T(8,128)(2,1)} %shard_map.113.rel_ref) | copy-start | bytes 2457604
  51.0 1.0 %copy-start.4 = (bf16[8,400,128]{2,1,0:T(8,128)(2,1)}, bf16[8,400,128]{2,1,0:T(8,128)(2,1)S(1)}, u32[]{:S(2)}) copy-start(bf16[8,400,128]{2,1,0:T(8,128)(2,1)S(1)} %get-tuple-element.33) | copy-start | bytes 2457604
  52.0 0.8 copy-start.7
  52.7 21.6 %all-to-all-start.2 = ((bf16[8,400,128]{2,1,0:T(8,128)(2,1)}), bf16[8,400,128]{2,1,0:T(8,128)(2,1)S(1)}, u32[]{:S(2)}, u32[]{:S(2)}) async-start(bf16[8,400,128]{2,1,0:T(8,128)(2,1)} %copy-done.4), calls=%async_computation.2 | async-start | bytes 1638400 | tf_op jit(solution)/shard_map/all_to_all | solution.py:224
  56.3 16.9 %copy-start.3 = (f32[400,512]{1,0:T(8,128)S(1)}, f32[400,512]{1,0:T(8,128)}, u32[]{:S(2)}) copy-start(f32[400,512]{1,0:T(8,128)} %get-tuple-element.34.tail_ref) | copy-start | bytes 2457604
  56.3 16.9 %copy-start.6 = (f32[1,512]{1,0:T(1,128)S(1)}, f32[1,512]{1,0:T(1,128)}, u32[]{:S(2)}) copy-start(f32[1,512]{1,0:T(1,128)} %get-tuple-element.35.state_ref) | copy-start | bytes 6148
  56.3 16.9 %collective-permute-start.1 = (bf16[400,512]{1,0:T(8,128)(2,1)}, bf16[400,512]{1,0:T(8,128)(2,1)S(1)}, u32[]{:S(2)}, u32[]{:S(2)}) collective-permute-start(bf16[400,512]{1,0:T(8,128)(2,1)} %copy-done.7), channel_id=1, source_target_pairs={{0,248},{8,0},{16,8},{24,16},{32,24},{40,32},{48,40},{56,48},{64,5... | collective-permute-start | bytes 1228808 | tf_op jit(solution)/shard_map/ppermute | solution.py:175
  59.5 1.2 %copy-start.1 = (f32[400,1024]{1,0:T(8,128)}, f32[400,1024]{1,0:T(8,128)S(1)}, u32[]{:S(2)}) copy-start(f32[400,1024]{1,0:T(8,128)S(1)} %get-tuple-element.41.head_ref) | copy-start | bytes 4915204
  74.3 16.7 %copy-start.2 = (f32[400,1024]{1,0:T(8,128)S(1)}, f32[400,1024]{1,0:T(8,128)}, u32[]{:S(2)}) copy-start(f32[400,1024]{1,0:T(8,128)} %copy-done.1) | copy-start | bytes 4915204
